TPU v7x, 256 devices: a whole 4x4x8 slice. The times are simulated.
256 devices in a mesh: tp: 16 (over x_lo, z), sc: 16 (over x_hi, y, core).
Axes of the slice: x: 4 (x_hi: 2, x_lo: 2; x = x_hi * 2 + x_lo), y: 4, z: 8, core: 2. Of those that a mesh axis runs over, the one named last changes fastest.
Arguments:
- upstream: bfloat16 [16, 1024, 5120], P('sc', 'tp'), may hold values from -6 to 6
- inputs: bfloat16 [16, 1024, 5120], P('sc', 'tp'), may hold values from -6 to 6
- gate_pre: bfloat16 [16, 1024, 12800], P('sc', None, 'tp'), may hold values from -8 to 8
- up_pre: bfloat16 [16, 1024, 12800], P('sc', None, 'tp'), may hold values from -6 to 6
- down_weight: bfloat16 [12800, 5120], P('tp'), may hold values from -0.0546875 to 0.0546875
- proj_in: bfloat16 [5120, 64], replicated, may hold values from -0.078125 to 0.078125
- proj_out: bfloat16 [12800, 64], P('tp'), may hold values from -0.15625 to 0.15625
- queries: bfloat16 [2048, 4096], P('sc'), may hold values from -0.099609375 to 0.099609375
- owner_table: int32 [16, 1024, 1], P('sc', 'tp'), may hold values from 0 to 15; in each aligned block of 64 rows (0 to 63, 64 to 127, ..., all dimensions but the last counted through in order) at most 8 rows name the same one
Outputs:
- influence: float32 [16, 1024, 128], P('sc', 'tp')
Inputs may be any that keep to these rules, and one draw needn't show every extreme that they name: `owner_table`: among the 64 rows of one device (aligned blocks in row order), no owner is named by more than 8 rows.
All inputs are finite; a program needn't handle non-finite values.
Results may differ from a plain program's by a relative error of at most 0.007.
Values may be sent and summed in bfloat16 or wider, within the bound.
No kernel may reach another device: no remote copies, remote signals or barrier semaphores. Data moves between devices by JAX's collectives and lax.ppermute only.
A program may use at most 128 MiB of HBM per device.

v0:
```python
import functools

import jax
import jax.numpy as jnp
from jax import lax
from jax.experimental import pallas as pl
from jax.experimental.pallas import tpu as pltpu
from jax.sharding import PartitionSpec as P

NZ, NY, CAP = 8, 4, 8
F32, BF16 = jnp.float32, jnp.bfloat16
SMALL = pl.CostEstimate(flops=1000, bytes_accessed=1000, transcendentals=0)


def tp_perm(flip_x, dz):
    return [
        (x * NZ + z, (x ^ flip_x) * NZ + (z + dz) % NZ) for x in range(2) for z in range(NZ)
    ]


def sc_perm(dy, flip_core):
    return [
        ((h * NY + y) * 2 + c, (h * NY + (y + dy) % NY) * 2 + (c ^ flip_core))
        for h in range(2)
        for y in range(NY)
        for c in range(2)
    ]


def along_tp(a, flip_x, dz):
    return lax.ppermute(a, "tp", tp_perm(flip_x, dz))


def along_sc(a, dy, flip_core):
    return lax.ppermute(a, "sc", sc_perm(dy, flip_core))


def across_x(a):
    pairs = []
    for x in range(2):
        for z in range(NZ):
            for s in range(16):
                pairs.append(((x * NZ + z) * 16 + s, ((1 - x) * NZ + z) * 16 + (s ^ 8)))
    return lax.ppermute(a, ("tp", "sc"), pairs)


def query_kernel(rows_ref, own_ref, other_ref, out_ref):
    count, wide = rows_ref.shape
    rows = rows_ref[...].astype(F32).reshape(count // (2 * CAP), 2, CAP, wide)
    first = lax.broadcasted_iota(jnp.int32, (count // 2, wide), 1) < wide // 2
    queries = own_ref.shape[0]
    half = count // 2

    def doubled(a):
        a = a.reshape(half, wide)
        zeros = jnp.zeros_like(a)
        return jnp.concatenate(
            [jnp.where(first, a, zeros), jnp.where(first, zeros, a)], axis=0
        ).astype(BF16)

    near, far = doubled(rows[:, 0]), doubled(rows[:, 1])
    dims = (((1,), (1,)), ((), ()))
    for p in range(own_ref.shape[1] // wide):
        cols = slice(p * wide, (p + 1) * wide)
        a = lax.dot_general(near, own_ref[:, cols], dims, preferred_element_type=F32)
        b = lax.dot_general(far, other_ref[:, cols], dims, preferred_element_type=F32)
        for k in range(2):
            both = jnp.stack(
                [
                    a[k * half : (k + 1) * half].reshape(half // CAP, CAP, queries),
                    b[k * half : (k + 1) * half].reshape(half // CAP, CAP, queries),
                ],
                axis=1,
            ).reshape(count, queries)
            out_ref[:, (2 * p + k) * queries : (2 * p + k + 1) * queries] = both.astype(BF16)


def contract_queries(rows, own, other):
    count, wide = rows.shape
    width = wide // 2
    queries, total = own.shape
    steps = 4
    return pl.pallas_call(
        query_kernel,
        grid=(steps,),
        in_specs=[
            pl.BlockSpec((count, wide), lambda p: (0, 0)),
            pl.BlockSpec((queries, total // steps), lambda p: (0, p)),
            pl.BlockSpec((queries, total // steps), lambda p: (0, p)),
        ],
        out_specs=pl.BlockSpec((count, queries * width // steps), lambda p: (0, p)),
        out_shape=jax.ShapeDtypeStruct((count, queries * width), BF16),
        compiler_params=pltpu.CompilerParams(vmem_limit_bytes=32 * 1024 * 1024),
        cost_estimate=SMALL,
        name="contract_queries",
    )(rows, own, other)


def score_kernel(place_ref, mats_ref, parts_ref, out_ref):
    half = parts_ref.shape[0] // NZ
    total = parts_ref[:half, :].astype(F32)
    for n in range(1, NZ):
        total = total + parts_ref[n * half : (n + 1) * half, :].astype(F32)
    count = total.shape[1] // 2
    total = jnp.concatenate([total[:, :count], total[:, count:]], axis=0)
    factor = total.astype(BF16).astype(F32).T
    queries = out_ref.shape[1]
    step = 8 * queries
    score = jnp.zeros(out_ref.shape, F32)
    for first in range(0, mats_ref.shape[1], step):
        mats = jnp.dot(
            place_ref[...], mats_ref[:, first : first + step], preferred_element_type=F32
        )
        for n in range(8):
            i = first // queries + n
            score = score + factor[:, i : i + 1] * mats[:, n * queries : (n + 1) * queries]
    out_ref[...] = score


def score_rows(place, mats, parts):
    rows = place.shape[0]
    queries = mats.shape[1] // (2 * parts.shape[0] // NZ)
    return pl.pallas_call(
        score_kernel,
        out_shape=jax.ShapeDtypeStruct((rows, queries), F32),
        compiler_params=pltpu.CompilerParams(vmem_limit_bytes=16 * 1024 * 1024),
        cost_estimate=SMALL,
        name="score_rows",
    )(place, mats, parts)


UNIT_STEPS = 5


def factor_kernel(at_ref, gate_ref, up_ref, out_ref):
    gate = gate_ref[...].astype(F32)
    sig = jax.nn.sigmoid(gate)
    out_ref[...] = (up_ref[...].astype(F32) * sig * (1.0 + gate * (1.0 - sig))).astype(BF16)


def gating_factor(at, gate, up):
    units, tokens = gate.shape
    column = tokens // 2
    block = units // UNIT_STEPS
    return pl.pallas_call(
        factor_kernel,
        grid_spec=pltpu.PrefetchScalarGridSpec(
            num_scalar_prefetch=1,
            grid=(UNIT_STEPS,),
            in_specs=[pl.BlockSpec((block, column), lambda p, at: (p, at[0]))] * 2,
            out_specs=pl.BlockSpec((block, column), lambda p, at: (p, 0)),
        ),
        out_shape=jax.ShapeDtypeStruct((units, column), BF16),
        compiler_params=pltpu.CompilerParams(vmem_limit_bytes=16 * 1024 * 1024),
        cost_estimate=SMALL,
        name="gating_factor",
    )(at, gate, up)


NT = (((1,), (1,)), ((), ()))


SMEM = pl.BlockSpec(memory_space=pltpu.SMEM)
VMEM = pl.BlockSpec(memory_space=pltpu.VMEM)
HBM = pl.BlockSpec(memory_space=pltpu.HBM)


OWN_CUTS = (512, 1024, 1792, 1792)


def multiply(weight, rows, hidden, first):
    term = lax.dot_general(weight, rows, NT, preferred_element_type=F32)
    if first:
        hidden[...] = term
    else:
        hidden[...] += term


def units_kernel(at_ref, p_own, p_other, f_own, f_other, rows_hbm, own_hbm, *refs):
    weights, (out_ref, rows, own, other, factor, hidden, sems) = refs[:-7], refs[-7:]
    per, _, deep = other.shape
    piece = deep // 2
    core = at_ref[per]
    copies = []

    def copy(src, dst):
        one = pltpu.make_async_copy(src, dst, sems.at[len(copies)])
        one.start()
        copies.append(one)

    rows_cols = []
    first = 0
    for deep_n in OWN_CUTS:
        cols = pl.ds(first, deep_n)
        copy(rows_hbm.at[:, cols], rows.at[:, cols])
        copy(own_hbm.at[:, cols], own.at[:, cols])
        rows_cols.append(slice(first, first + deep_n))
        first += deep_n
    copy(f_own, factor.at[0])
    for n in range(per):
        for f in range(2):
            side = pl.ds(pl.multiple_of((core if f == 0 else 1 - core) * piece, 128), piece)
            copy(weights[f * per + n], other.at[n, :, side])
    copy(f_other, factor.at[1])
    copies = iter(copies)

    def project(k, proj):
        next(copies).wait()
        grad = (hidden[...] * factor[k].astype(F32)).astype(BF16)
        return lax.dot_general(
            proj[...], grad, (((0,), (0,)), ((), ())), preferred_element_type=F32
        )

    for n, cols in enumerate(rows_cols):
        next(copies).wait()
        next(copies).wait()
        multiply(own[:, cols], rows[:, cols], hidden, n == 0)
    total = project(0, p_own)
    for n in range(per):
        next(copies).wait()
        next(copies).wait()
        cols = pl.ds(pl.multiple_of(at_ref[n] * deep, 128), deep)
        multiply(other[n], rows[:, cols], hidden, n == 0)
    total = total + project(1, p_other)
    half = total.shape[0] // 2
    count = total.shape[1] // NZ
    for n in range(NZ):
        part = total[:, n * count : (n + 1) * count]
        part = jnp.concatenate([part[:half], part[half:]], axis=1)
        out_ref[n * half : (n + 1) * half, :] = part.astype(BF16)


def sum_units(at, p_own, p_other, f_own, f_other, rows, own, weights):
    tokens, depth = rows.shape
    units, width = p_own.shape
    return pl.pallas_call(
        units_kernel,
        in_specs=[SMEM, VMEM, VMEM] + [HBM] * (4 + len(weights)),
        out_specs=VMEM,
        out_shape=jax.ShapeDtypeStruct((NZ * width // 2, 2 * tokens // NZ), BF16),
        scratch_shapes=[
            pltpu.VMEM((tokens, depth), BF16),
            pltpu.VMEM((units, depth), BF16),
            pltpu.VMEM((NY, units, depth // NY), BF16),
            pltpu.VMEM((2, units, tokens), BF16),
            pltpu.VMEM((units, tokens), F32),
            pltpu.SemaphoreType.DMA((2 * len(OWN_CUTS) + 2 + len(weights),)),
        ],
        compiler_params=pltpu.CompilerParams(vmem_limit_bytes=56 * 1024 * 1024),
        cost_estimate=SMALL,
        name="sum_units",
    )(at, p_own, p_other, f_own, f_other, rows, own, *weights)


def together(*arrays):
    return lax.optimization_barrier(arrays)


def body(upstream, inputs, gate_pre, up_pre, down_weight, proj_in, proj_out, queries, owner_table):
    rows_own = upstream[0]
    count, depth = rows_own.shape
    units = down_weight.shape[0]
    tp, sc = lax.axis_index("tp"), lax.axis_index("sc")
    x_lo, z = tp // NZ, tp % NZ
    x_hi, y, core = sc // (2 * NY), (sc // 2) % NY, sc % 2

    columns = [list(range(NZ)), list(range(NZ, 2 * NZ))]
    rows = lax.all_gather(rows_own, "tp", axis=0, tiled=True, axis_index_groups=columns)

    piece = depth // (2 * NY)

    def eighth(column, count=units):
        return lax.dynamic_slice(down_weight, (0, column), (count, piece))

    here = along_tp(eighth((y * 2 + core) * piece), 1, 0)
    proj_other = along_tp(proj_out, 1, 0)
    other_queries = across_x(queries)
    gate, up_rows = gate_pre[0].T, up_pre[0].T
    factor_other = gating_factor(jnp.stack([1 - x_lo]), gate, up_rows)
    factor_own = gating_factor(jnp.stack([x_lo]), gate, up_rows)

    in_factor = jnp.dot(inputs[0], proj_in, preferred_element_type=F32).astype(BF16)
    at_far, in_factor = together((((y + 2) % NY) * 2 + core) * piece, in_factor)
    second = eighth(at_far)
    owners = owner_table[0, :, 0]
    ids = jnp.arange(count, dtype=jnp.int32)
    same = (owners[:, None] == owners[None, :]) & (ids[:, None] > ids[None, :])
    rank = jnp.sum(same.astype(jnp.int32), axis=1)
    groups = 2 * NY
    slot = (owners % groups) * (2 * CAP) + ((owners // groups) ^ x_hi) * CAP + rank
    slots = groups * 2 * CAP
    place = (slot[:, None] == jnp.arange(slots, dtype=jnp.int32)[None, :]).astype(BF16)
    packed = lax.dot_general(
        place,
        jnp.concatenate([in_factor, in_factor], axis=1),
        (((0,), (0,)), ((), ())),
        preferred_element_type=F32,
    ).astype(BF16)
    near = [list(range(groups)), list(range(groups, 2 * groups))]
    arrived = lax.all_to_all(
        packed, "sc", split_axis=0, concat_axis=0, tiled=True, axis_index_groups=near
    )

    here, arrived, factor_other, factor_own, second = together(
        here, arrived, factor_other, factor_own, second
    )
    before, after = along_sc(here, 1, 0), along_sc(here, -1, 0)
    factor_other = along_tp(factor_other, 1, 0)
    mats = contract_queries(arrived, queries, other_queries)

    factor_other, mats, second, proj_other = together(factor_other, mats, second, proj_other)
    far = along_tp(second, 1, 0)
    before, after, mats = together(before, after, mats)
    held = [here, before, after, far]
    flipped = [along_sc(a, 0, 1) for a in held]
    mats = lax.all_to_all(
        mats, "sc", split_axis=0, concat_axis=0, tiled=True, axis_index_groups=near
    )
    at = jnp.stack([(y + dy) % NY for dy in (0, -1, 1, 2)] + [core]).astype(jnp.int32)
    parts = sum_units(
        at,
        proj_out,
        proj_other,
        factor_own,
        factor_other,
        rows,
        down_weight,
        held + flipped,
    )
    parts, mats = together(parts, mats)
    parts = lax.all_to_all(
        parts, "tp", split_axis=0, concat_axis=0, tiled=True, axis_index_groups=columns
    )
    return score_rows(place, mats, parts)[None]


def solution(mesh):
    placed = (
        P("sc", "tp", None),
        P("sc", "tp", None),
        P("sc", None, "tp"),
        P("sc", None, "tp"),
        P("tp", None),
        P(),
        P("tp", None),
        P("sc", None),
        P("sc", "tp", None),
    )
    return jax.shard_map(
        body, mesh=mesh, in_specs=placed, out_specs=P("sc", "tp", None), check_vma=False
    )
```

profile of v0, /device:TPU:6, one launch (start us, length us, event | category | flops | bytes accessed | tf_op | source)
XLA Modules:
  0.0 126.2 jit_solution(10712505086210931727)
XLA Ops:
  7.6 1.4 %convolution_convert_fusion.1 = bf16[64,64]{1,0:T(8,128)(2,1)S(1)} fusion(bf16[5120,64]{0,1:T(8,128)(2,1)S(1)} %copy-done, bf16[1,64,5120]{2,1,0:T(8,128)(2,1)} %param.10), kind=kOutput, calls=%fused_computation.1 | convolution fusion | flops 41947136 | bytes 1318912 | tf_op jit(solution)/shard_map/dot_general | solution.py:282
  9.1 3.6 %constant_dynamic-slice_fusion = (bf16[800,640]{1,0:T(8,128)(2,1)}, bf16[800,640]{1,0:T(8,128)(2,1)}) fusion(bf16[800,5120]{1,0:T(8,128)(2,1)} %own_hbm.1, s32[]{:T(128)S(6)} %select_n.76, s32[]{:T(128)S(6)} %select_n.74), kind=kLoop, calls=%fused_computation.20 | loop fusion | bytes 4096008 | tf_op jit(solution)/shard_map/dynamic_slice | solution.py:273
  13.5 1.5 %collective-permute-start.2 = (bf16[128,4096]{1,0:T(8,128)(2,1)S(1)}, bf16[128,4096]{1,0:T(8,128)(2,1)}, u32[]{:S(2)}, u32[]{:S(2)}) collective-permute-start(bf16[128,4096]{1,0:T(8,128)(2,1)S(1)} %copy-done.5), channel_id=1, source_target_pairs={{0,136},{1,137},{2,138},{3,139},{4,140},{5,141},{6,142},{7,143},{8... | collective-permute-start | bytes 3145736 | tf_op jit(solution)/shard_map/ppermute | solution.py:44
  15.2 0.9 convolution_convert_fusion
  16.1 4.1 %all-to-all-start = ((bf16[8,16,128]{2,1,0:T(8,128)(2,1)}), bf16[8,16,128]{2,1,0:T(8,128)(2,1)S(1)}, u32[]{:S(2)}, u32[]{:S(2)}) async-start(bf16[8,16,128]{2,1,0:T(8,128)(2,1)} %bitcast.7), calls=%async_computation | async-start | bytes 65536 | tf_op jit(solution)/shard_map/all_to_all | solution.py:300
  20.2 1.4 %copy-done.2 = bf16[1,1024,800]{1,2,0:T(8,128)(2,1)S(1)} copy-done((bf16[1,1024,800]{1,2,0:T(8,128)(2,1)S(1)}, bf16[1,1024,800]{1,2,0:T(8,128)(2,1)}, u32[]{:S(2)}) %copy-start.2) | copy-done | bytes 1638424
  22.5 1.0 copy-done.6
  24.3 0.9 copy-done.4
  25.7 11.7 %collective-permute-done.refs_0_ = bf16[800,640]{1,0:T(8,128)(2,1)} collective-permute-done((bf16[800,640]{1,0:T(8,128)(2,1)}, bf16[800,640]{1,0:T(8,128)(2,1)}, u32[]{:S(2)}, u32[]{:S(2)}) %collective-permute-start) | collective-permute-done | bytes 1024032 | tf_op jit(solution)/shard_map/ppermute | solution.py:31
  37.3 0.8 collective-permute-start.1
  38.2 1.5 %collective-permute-start.4 = (bf16[800,640]{1,0:T(8,128)(2,1)}, bf16[800,640]{1,0:T(8,128)(2,1)}, u32[]{:S(2)}, u32[]{:S(2)}) collective-permute-start(bf16[800,640]{1,0:T(8,128)(2,1)} %collective-permute-done.refs_0_), channel_id=1, source_target_pairs={{0,2},{1,3},{2,4},{3,5},{4,6},{5,7},{6,0},{7,1},{8,10},{9,11},{10,... | collective-permute-start | bytes 3072008 | tf_op jit(solution)/shard_map/ppermute | solution.py:35
  39.7 1.7 %collective-permute-start.5 = (bf16[800,640]{1,0:T(8,128)(2,1)}, bf16[800,640]{1,0:T(8,128)(2,1)}, u32[]{:S(2)}, u32[]{:S(2)}) collective-permute-start(bf16[800,640]{1,0:T(8,128)(2,1)} %collective-permute-done.refs_0_), channel_id=1, source_target_pairs={{0,6},{1,7},{2,0},{3,1},{4,2},{5,3},{6,4},{7,5},{8,14},{9,15},{10,... | collective-permute-start | bytes 3072008 | tf_op jit(solution)/shard_map/ppermute | solution.py:35
  41.6 1.3 %collective-permute-start.3 = (bf16[800,64]{1,0:T(8,128)(2,1)S(1)}, bf16[800,64]{1,0:T(8,128)(2,1)S(1)}, u32[]{:S(2)}, u32[]{:S(2)}) collective-permute-start(bf16[800,64]{1,0:T(8,128)(2,1)S(1)} %copy.13.p_own), channel_id=1, source_target_pairs={{0,128},{16,144},{32,160},{48,176},{64,192},{80,208},{96,224},{112... | collective-permute-start | bytes 307208 | tf_op jit(solution)/shard_map/ppermute | solution.py:31
  42.9 4.6 %contract_queries.1 = bf16[128,8192]{1,0:T(8,128)(2,1)} custom-call(bf16[128,128]{1,0:T(8,128)(2,1)S(1)} %bitcast.33, bf16[128,4096]{1,0:T(8,128)(2,1)S(1)} %copy-done.5, bf16[128,4096]{1,0:T(8,128)(2,1)} %collective-permute-done.2.other_ref), custom_call_target="tpu_custom_call" | custom-call | flops 1000 | bytes 1000 | tf_op jit(solution)/shard_map/contract_queries/pallas_call | solution.py:83
  47.5 13.6 %collective-permute-done.3.p_other = bf16[800,64]{1,0:T(8,128)(2,1)S(1)} collective-permute-done((bf16[800,64]{1,0:T(8,128)(2,1)S(1)}, bf16[800,64]{1,0:T(8,128)(2,1)S(1)}, u32[]{:S(2)}, u32[]{:S(2)}) %collective-permute-start.3) | collective-permute-done | bytes 102432 | tf_op jit(solution)/shard_map/ppermute | solution.py:31
  61.1 0.8 collective-permute-start.6
  61.9 1.1 collective-permute-done.4.refs_1_
  63.0 4.2 %all-to-all-start.1 = ((bf16[8,16,8192]{2,1,0:T(8,128)(2,1)}), bf16[8,16,8192]{2,1,0:T(8,128)(2,1)S(1)}, u32[]{:S(2)}, u32[]{:S(2)}) async-start(bf16[8,16,8192]{2,1,0:T(8,128)(2,1)} %bitcast.18), calls=%async_computation.1 | async-start | bytes 4194304 | tf_op jit(solution)/shard_map/all_to_all | solution.py:316
  68.2 15.8 %collective-permute-done.6.refs_3_ = bf16[800,640]{1,0:T(8,128)(2,1)} collective-permute-done((bf16[800,640]{1,0:T(8,128)(2,1)}, bf16[800,640]{1,0:T(8,128)(2,1)}, u32[]{:S(2)}, u32[]{:S(2)}) %collective-permute-start.6) | collective-permute-done | bytes 1024032 | tf_op jit(solution)/shard_map/ppermute | solution.py:31
  84.7 2.3 %collective-permute-done.10.refs_7_ = bf16[800,640]{1,0:T(8,128)(2,1)} collective-permute-done((bf16[800,640]{1,0:T(8,128)(2,1)}, bf16[800,640]{1,0:T(8,128)(2,1)}, u32[]{:S(2)}, u32[]{:S(2)}) %collective-permute-start.10) | collective-permute-done | bytes 1024032 | tf_op jit(solution)/shard_map/ppermute | solution.py:35
  87.0 14.2 %sum_units.1 = bf16[256,128]{1,0:T(8,128)(2,1)} custom-call(s32[5]{0:T(128)} %stack.29.at_ref, bf16[800,64]{1,0:T(8,128)(2,1)} %copy-done.7, bf16[800,64]{1,0:T(8,128)(2,1)} %copy-done.8, bf16[800,512]{1,0:T(8,128)(2,1)} %copy-done.4, bf16[800,512]{1,0:T(8,128)(2,1)} %collective-permute-done.1.f_other, bf16[512,5120]{1,0:T(8,128)(2,1)} %bitcast.34, ...), custom_call_target="tpu_custom_call" | custom-call | flops 1000 | bytes 1000 | tf_op jit(solution)/shard_map/sum_units/pallas_call | solution.py:236
  101.3 8.5 %all-to-all-start.2 = ((bf16[8,32,128]{2,1,0:T(8,128)(2,1)}), bf16[8,32,128]{2,1,0:T(8,128)(2,1)S(1)}, u32[]{:S(2)}, u32[]{:S(2)}) async-start(bf16[8,32,128]{2,1,0:T(8,128)(2,1)} %bitcast.35), calls=%async_computation.2 | async-start | bytes 131072 | tf_op jit(solution)/shard_map/all_to_all | solution.py:331
  109.8 8.3 %all-to-all-done.2 = bf16[8,32,128]{2,1,0:T(8,128)(2,1)S(1)} async-done(((bf16[8,32,128]{2,1,0:T(8,128)(2,1)}), bf16[8,32,128]{2,1,0:T(8,128)(2,1)S(1)}, u32[]{:S(2)}, u32[]{:S(2)}) %all-to-all-start.2) | async-done | bytes 65568 | tf_op jit(solution)/shard_map/all_to_all | solution.py:331
  118.1 1.2 score_rows.1
  (42 shorter events, 6.1 us)
Async XLA Ops:
  6.5 1.1 copy-start
  6.5 80.5 %all-gather.3.cloned.1.call-start = ((), (), s32[]{:S(2)}) async-start(), calls=%async_computation.3 | async-start | bytes 5898240 | tf_op jit(solution)/shard_map/all_gather | solution.py:268
  9.0 4.4 %copy-start.5 = (bf16[128,4096]{1,0:T(8,128)(2,1)S(1)}, bf16[128,4096]{1,0:T(8,128)(2,1)}, u32[]{:S(2)}) copy-start(bf16[128,4096]{1,0:T(8,128)(2,1)} %own_ref.1) | copy-start | bytes 3145732
  9.0 5.9 %copy-start.10 = (s32[1,64,1]{1,2,0:T(1,128)S(1)}, s32[1,64,1]{1,2,0:T(1,128)}, u32[]{:S(2)}) copy-start(s32[1,64,1]{1,2,0:T(1,128)} %param.17) | copy-start | bytes 772
  9.1 11.1 %copy-start.1 = (bf16[1,1024,800]{1,2,0:T(8,128)(2,1)S(1)}, bf16[1,1024,800]{1,2,0:T(8,128)(2,1)}, u32[]{:S(2)}) copy-start(bf16[1,1024,800]{1,2,0:T(8,128)(2,1)} %param.11) | copy-start | bytes 4915204
  12.7 24.7 %collective-permute-start = (bf16[800,640]{1,0:T(8,128)(2,1)}, bf16[800,640]{1,0:T(8,128)(2,1)}, u32[]{:S(2)}, u32[]{:S(2)}) collective-permute-start(bf16[800,640]{1,0:T(8,128)(2,1)} %get-tuple-element.38), channel_id=1, source_target_pairs={{0,128},{16,144},{32,160},{48,176},{64,192},{80,208},{96,224},{112... | collective-permute-start | bytes 3072008 | tf_op jit(solution)/shard_map/ppermute | solution.py:31
  13.5 29.4 %collective-permute-start.2 = (bf16[128,4096]{1,0:T(8,128)(2,1)S(1)}, bf16[128,4096]{1,0:T(8,128)(2,1)}, u32[]{:S(2)}, u32[]{:S(2)}) collective-permute-start(bf16[128,4096]{1,0:T(8,128)(2,1)S(1)} %copy-done.5), channel_id=1, source_target_pairs={{0,136},{1,137},{2,138},{3,139},{4,140},{5,141},{6,142},{7,143},{8... | collective-permute-start | bytes 3145736 | tf_op jit(solution)/shard_map/ppermute | solution.py:44
  16.1 9.6 %all-to-all-start = ((bf16[8,16,128]{2,1,0:T(8,128)(2,1)}), bf16[8,16,128]{2,1,0:T(8,128)(2,1)S(1)}, u32[]{:S(2)}, u32[]{:S(2)}) async-start(bf16[8,16,128]{2,1,0:T(8,128)(2,1)} %bitcast.7), calls=%async_computation | async-start | bytes 65536 | tf_op jit(solution)/shard_map/all_to_all | solution.py:300
  20.2 1.4 %copy-start.2 = (bf16[1,1024,800]{1,2,0:T(8,128)(2,1)S(1)}, bf16[1,1024,800]{1,2,0:T(8,128)(2,1)}, u32[]{:S(2)}) copy-start(bf16[1,1024,800]{1,2,0:T(8,128)(2,1)} %param.12) | copy-start | bytes 4915204
  21.6 1.8 %copy-start.3 = (bf16[1,1024,800]{1,2,0:T(8,128)(2,1)S(1)}, bf16[1,1024,800]{1,2,0:T(8,128)(2,1)}, u32[]{:S(2)}) copy-start(bf16[1,1024,800]{1,2,0:T(8,128)(2,1)} %param.12) | copy-start | bytes 4915204
  23.4 18.0 %copy-start.9 = (bf16[800,64]{0,1:T(8,128)(2,1)S(1)}, bf16[800,64]{0,1:T(8,128)(2,1)}, u32[]{:S(2)}) copy-start(bf16[800,64]{0,1:T(8,128)(2,1)} %param.15) | copy-start | bytes 307204
  37.3 23.7 %collective-permute-start.1 = (bf16[800,512]{1,0:T(8,128)(2,1)}, bf16[800,512]{1,0:T(8,128)(2,1)}, u32[]{:S(2)}, u32[]{:S(2)}) collective-permute-start(bf16[800,512]{1,0:T(8,128)(2,1)} %copy-done.6), channel_id=1, source_target_pairs={{0,128},{16,144},{32,160},{48,176},{64,192},{80,208},{96,224},{112... | collective-permute-start | bytes 2457608 | tf_op jit(solution)/shard_map/ppermute | solution.py:31
  38.2 24.8 %collective-permute-start.4 = (bf16[800,640]{1,0:T(8,128)(2,1)}, bf16[800,640]{1,0:T(8,128)(2,1)}, u32[]{:S(2)}, u32[]{:S(2)}) collective-permute-start(bf16[800,640]{1,0:T(8,128)(2,1)} %collective-permute-done.refs_0_), channel_id=1, source_target_pairs={{0,2},{1,3},{2,4},{3,5},{4,6},{5,7},{6,0},{7,1},{8,10},{9,11},{10,... | collective-permute-start | bytes 3072008 | tf_op jit(solution)/shard_map/ppermute | solution.py:35
  39.7 23.3 %collective-permute-start.5 = (bf16[800,640]{1,0:T(8,128)(2,1)}, bf16[800,640]{1,0:T(8,128)(2,1)}, u32[]{:S(2)}, u32[]{:S(2)}) collective-permute-start(bf16[800,640]{1,0:T(8,128)(2,1)} %collective-permute-done.refs_0_), channel_id=1, source_target_pairs={{0,6},{1,7},{2,0},{3,1},{4,2},{5,3},{6,4},{7,5},{8,14},{9,15},{10,... | collective-permute-start | bytes 3072008 | tf_op jit(solution)/shard_map/ppermute | solution.py:35
  41.6 5.9 %copy-start.7 = (bf16[800,64]{1,0:T(8,128)(2,1)}, bf16[800,64]{1,0:T(8,128)(2,1)S(1)}, u32[]{:S(2)}) copy-start(bf16[800,64]{1,0:T(8,128)(2,1)S(1)} %copy.13.p_own) | copy-start | bytes 307204
  41.6 19.5 %collective-permute-start.3 = (bf16[800,64]{1,0:T(8,128)(2,1)S(1)}, bf16[800,64]{1,0:T(8,128)(2,1)S(1)}, u32[]{:S(2)}, u32[]{:S(2)}) collective-permute-start(bf16[800,64]{1,0:T(8,128)(2,1)S(1)} %copy.13.p_own), channel_id=1, source_target_pairs={{0,128},{16,144},{32,160},{48,176},{64,192},{80,208},{96,224},{112... | collective-permute-start | bytes 307208 | tf_op jit(solution)/shard_map/ppermute | solution.py:31
  61.1 1.9 %copy-start.8 = (bf16[800,64]{1,0:T(8,128)(2,1)}, bf16[800,64]{1,0:T(8,128)(2,1)S(1)}, u32[]{:S(2)}) copy-start(bf16[800,64]{1,0:T(8,128)(2,1)S(1)} %collective-permute-done.3.p_other) | copy-start | bytes 307204
  61.1 23.0 %collective-permute-start.6 = (bf16[800,640]{1,0:T(8,128)(2,1)}, bf16[800,640]{1,0:T(8,128)(2,1)}, u32[]{:S(2)}, u32[]{:S(2)}) collective-permute-start(bf16[800,640]{1,0:T(8,128)(2,1)} %get-tuple-element.33), channel_id=1, source_target_pairs={{0,128},{16,144},{32,160},{48,176},{64,192},{80,208},{96,224},{112... | collective-permute-start | bytes 3072008 | tf_op jit(solution)/shard_map/ppermute | solution.py:31
  63.0 38.2 %all-to-all-start.1 = ((bf16[8,16,8192]{2,1,0:T(8,128)(2,1)}), bf16[8,16,8192]{2,1,0:T(8,128)(2,1)S(1)}, u32[]{:S(2)}, u32[]{:S(2)}) async-start(bf16[8,16,8192]{2,1,0:T(8,128)(2,1)} %bitcast.18), calls=%async_computation.1 | async-start | bytes 4194304 | tf_op jit(solution)/shard_map/all_to_all | solution.py:316
  67.2 17.5 %collective-permute-start.7 = (bf16[800,640]{1,0:T(8,128)(2,1)}, bf16[800,640]{1,0:T(8,128)(2,1)}, u32[]{:S(2)}, u32[]{:S(2)}) collective-permute-start(bf16[800,640]{1,0:T(8,128)(2,1)} %collective-permute-done.refs_0_), channel_id=1, source_target_pairs={{0,1},{1,0},{2,3},{3,2},{4,5},{5,4},{6,7},{7,6},{8,9},{9,8},{10,11... | collective-permute-start | bytes 3072008 | tf_op jit(solution)/shard_map/ppermute | solution.py:35
  67.7 17.0 %collective-permute-start.8 = (bf16[800,640]{1,0:T(8,128)(2,1)}, bf16[800,640]{1,0:T(8,128)(2,1)}, u32[]{:S(2)}, u32[]{:S(2)}) collective-permute-start(bf16[800,640]{1,0:T(8,128)(2,1)} %collective-permute-done.4.refs_1_), channel_id=1, source_target_pairs={{0,1},{1,0},{2,3},{3,2},{4,5},{5,4},{6,7},{7,6},{8,9},{9,8},{10,11... | collective-permute-start | bytes 3072008 | tf_op jit(solution)/shard_map/ppermute | solution.py:35
  67.7 17.0 %collective-permute-start.9 = (bf16[800,640]{1,0:T(8,128)(2,1)}, bf16[800,640]{1,0:T(8,128)(2,1)}, u32[]{:S(2)}, u32[]{:S(2)}) collective-permute-start(bf16[800,640]{1,0:T(8,128)(2,1)} %collective-permute-done.5.refs_2_), channel_id=1, source_target_pairs={{0,1},{1,0},{2,3},{3,2},{4,5},{5,4},{6,7},{7,6},{8,9},{9,8},{10,11... | collective-permute-start | bytes 3072008 | tf_op jit(solution)/shard_map/ppermute | solution.py:35
  84.1 3.0 %collective-permute-start.10 = (bf16[800,640]{1,0:T(8,128)(2,1)}, bf16[800,640]{1,0:T(8,128)(2,1)}, u32[]{:S(2)}, u32[]{:S(2)}) collective-permute-start(bf16[800,640]{1,0:T(8,128)(2,1)} %collective-permute-done.6.refs_3_), channel_id=1, source_target_pairs={{0,1},{1,0},{2,3},{3,2},{4,5},{5,4},{6,7},{7,6},{8,9},{9,8},{10,11... | collective-permute-start | bytes 3072008 | tf_op jit(solution)/shard_map/ppermute | solution.py:35
  101.3 16.9 %all-to-all-start.2 = ((bf16[8,32,128]{2,1,0:T(8,128)(2,1)}), bf16[8,32,128]{2,1,0:T(8,128)(2,1)S(1)}, u32[]{:S(2)}, u32[]{:S(2)}) async-start(bf16[8,32,128]{2,1,0:T(8,128)(2,1)} %bitcast.35), calls=%async_computation.2 | async-start | bytes 131072 | tf_op jit(solution)/shard_map/all_to_all | solution.py:331
  (2 other events, 1.9 us)
Sparse Core Ops, SparseCore 0:
  9.1 67.5 all-gather.2
where the time goes:
time: 127 us; the launch traced here: 126 us
  waiting for transfers between devices  54 us (43%)
  starting transfers between devices  26.4 us (21%)
  Pallas kernels  21.7 us (17%)
  between operations  13.6 us (11%)
  local copies, waits for them, and re-layouts  7.98 us (6%)
  matrix products  2.31 us (2%)
    ppermute x4, waiting for transfers between devices, along_tp(): return lax.ppermute(a, 'tp', tp_perm(flip_x, dz))  41.1 us
    pallas_call x1, Pallas kernels, sum_units(): pl.pallas_call(units_kernel, in_specs=[SMEM, VMEM, VMEM] + [HBM] * (4 + l...  14.2 us
    all_to_all x1, starting transfers between devices, body(): lax.all_to_all(parts, 'tp', split_axis=0, concat_axis=0, tiled=True, axis...  8.49 us
    all_to_all x1, waiting for transfers between devices, body(): lax.all_to_all(parts, 'tp', split_axis=0, concat_axis=0, tiled=True, axis...  8.3 us
    pallas_call x1, Pallas kernels, contract_queries(): pl.pallas_call(query_kernel, grid=(steps,), in_specs=[pl.BlockSpec((count...  4.62 us
    ppermute x6, starting transfers between devices, along_sc(): return lax.ppermute(a, 'sc', sc_perm(dy, flip_core))  4.25 us
    all_to_all x1, starting transfers between devices, body(): lax.all_to_all(mats, 'sc', split_axis=0, concat_axis=0, tiled=True, axis_...  4.23 us
    all_to_all x1, starting transfers between devices, body(): lax.all_to_all(packed, 'sc', split_axis=0, concat_axis=0, tiled=True, axi...  4.14 us
  transfers between devices with their start and end apart: 15, of which 7 were waited for; matrix products, arithmetic and copies ran while one was open for 5% of the time, Pallas kernels for 16%

commit v1 on v0

--- a/solution.py
+++ b/solution.py
@@ -135,7 +135,8 @@
 def factor_kernel(at_ref, gate_ref, up_ref, out_ref):
     gate = gate_ref[...].astype(F32)
     sig = jax.nn.sigmoid(gate)
-    out_ref[...] = (up_ref[...].astype(F32) * sig * (1.0 + gate * (1.0 - sig))).astype(BF16)
+    out = up_ref[...].astype(F32) * sig * (1.0 + gate * (1.0 - sig))
+    out_ref[...] = out.astype(BF16)
 
 
 def gating_factor(at, gate, up):
@@ -165,9 +166,6 @@
 HBM = pl.BlockSpec(memory_space=pltpu.HBM)
 
 
-OWN_CUTS = (512, 1024, 1792, 1792)
-
-
 def multiply(weight, rows, hidden, first):
     term = lax.dot_general(weight, rows, NT, preferred_element_type=F32)
     if first:
@@ -176,52 +174,52 @@
         hidden[...] += term
 
 
-def units_kernel(at_ref, p_own, p_other, f_own, f_other, rows_hbm, own_hbm, *refs):
+def project(hidden, factor, proj):
+    grad = (hidden * factor.astype(F32)).astype(BF16)
+    return lax.dot_general(proj, grad, (((0,), (0,)), ((), ())), preferred_element_type=F32)
+
+
+def units_kernel(at_ref, p_own, p_other, f_own, f_other, own_hbm, rows_hbm, *refs):
     weights, (out_ref, rows, own, other, factor, hidden, sems) = refs[:-7], refs[-7:]
     per, _, deep = other.shape
-    piece = deep // 2
-    core = at_ref[per]
-    copies = []
-
-    def copy(src, dst):
-        one = pltpu.make_async_copy(src, dst, sems.at[len(copies)])
-        one.start()
-        copies.append(one)
-
-    rows_cols = []
-    first = 0
-    for deep_n in OWN_CUTS:
-        cols = pl.ds(first, deep_n)
-        copy(rows_hbm.at[:, cols], rows.at[:, cols])
-        copy(own_hbm.at[:, cols], own.at[:, cols])
-        rows_cols.append(slice(first, first + deep_n))
-        first += deep_n
-    copy(f_own, factor.at[0])
+    side = deep // 2
+    sides = [pl.ds(pl.multiple_of(at_ref[per + f] * side, 128), side) for f in range(2)]
+    groups = []
     for n in range(per):
-        for f in range(2):
-            side = pl.ds(pl.multiple_of((core if f == 0 else 1 - core) * piece, 128), piece)
-            copy(weights[f * per + n], other.at[n, :, side])
-    copy(f_other, factor.at[1])
-    copies = iter(copies)
-
-    def project(k, proj):
-        next(copies).wait()
-        grad = (hidden[...] * factor[k].astype(F32)).astype(BF16)
-        return lax.dot_general(
-            proj[...], grad, (((0,), (0,)), ((), ())), preferred_element_type=F32
-        )
-
-    for n, cols in enumerate(rows_cols):
-        next(copies).wait()
-        next(copies).wait()
-        multiply(own[:, cols], rows[:, cols], hidden, n == 0)
-    total = project(0, p_own)
+        columns = pl.ds(n * deep, deep)
+        group = [(own_hbm.at[:, columns], own.at[n])]
+        group.append((rows_hbm.at[:, columns], rows.at[n]))
+        groups.append(group)
+    groups[-1].append((f_own, factor.at[0]))
     for n in range(per):
-        next(copies).wait()
-        next(copies).wait()
-        cols = pl.ds(pl.multiple_of(at_ref[n] * deep, 128), deep)
-        multiply(other[n], rows[:, cols], hidden, n == 0)
-    total = total + project(1, p_other)
+        groups.append([(weights[2 * n + f], other.at[n, :, sides[f]]) for f in range(2)])
+    groups[-1].append((f_other, factor.at[1]))
+    started = []
+    count = 0
+    for group in groups:
+        started.append([])
+        for src, dst in group:
+            started[-1].append(pltpu.make_async_copy(src, dst, sems.at[count]))
+            count += 1
+
+    ahead = 3
+    for group in started[:ahead]:
+        for one in group:
+            one.start()
+    total = None
+    for k, group in enumerate(started):
+        for one in group:
+            one.wait()
+        for one in started[k + ahead] if k + ahead < len(started) else []:
+            one.start()
+        n = k % per
+        if k < per:
+            multiply(own[n], rows[n], hidden, n == 0)
+        else:
+            multiply(other[n], rows[at_ref[n]], hidden, n == 0)
+        if k == per - 1:
+            total = project(hidden[...], factor[0], p_own[...])
+    total = total + project(hidden[...], factor[1], p_other[...])
     half = total.shape[0] // 2
     count = total.shape[1] // NZ
     for n in range(NZ):
@@ -230,26 +228,28 @@
         out_ref[n * half : (n + 1) * half, :] = part.astype(BF16)
 
 
-def sum_units(at, p_own, p_other, f_own, f_other, rows, own, weights):
-    tokens, depth = rows.shape
-    units, width = p_own.shape
+def sum_units(at, p_own, p_other, f_own, f_other, own, rows, weights):
+    units, depth = own.shape
+    tokens, width = f_own.shape[1], p_own.shape[1]
+    deep = depth // NY
+    copies = 2 * NY + 2 + len(weights)
     return pl.pallas_call(
         units_kernel,
         in_specs=[SMEM, VMEM, VMEM] + [HBM] * (4 + len(weights)),
         out_specs=VMEM,
         out_shape=jax.ShapeDtypeStruct((NZ * width // 2, 2 * tokens // NZ), BF16),
         scratch_shapes=[
-            pltpu.VMEM((tokens, depth), BF16),
-            pltpu.VMEM((units, depth), BF16),
-            pltpu.VMEM((NY, units, depth // NY), BF16),
+            pltpu.VMEM((NY, tokens, deep), BF16),
+            pltpu.VMEM((NY, units, deep), BF16),
+            pltpu.VMEM((NY, units, deep), BF16),
             pltpu.VMEM((2, units, tokens), BF16),
             pltpu.VMEM((units, tokens), F32),
-            pltpu.SemaphoreType.DMA((2 * len(OWN_CUTS) + 2 + len(weights),)),
+            pltpu.SemaphoreType.DMA((copies,)),
         ],
         compiler_params=pltpu.CompilerParams(vmem_limit_bytes=56 * 1024 * 1024),
         cost_estimate=SMALL,
         name="sum_units",
-    )(at, p_own, p_other, f_own, f_other, rows, own, *weights)
+    )(at, p_own, p_other, f_own, f_other, own, rows, *weights)
 
 
 def together(*arrays):
@@ -265,23 +265,19 @@
     x_hi, y, core = sc // (2 * NY), (sc // 2) % NY, sc % 2
 
     columns = [list(range(NZ)), list(range(NZ, 2 * NZ))]
+
+    piece = depth // (2 * NY)
     rows = lax.all_gather(rows_own, "tp", axis=0, tiled=True, axis_index_groups=columns)
 
-    piece = depth // (2 * NY)
-
-    def eighth(column, count=units):
-        return lax.dynamic_slice(down_weight, (0, column), (count, piece))
-
-    here = along_tp(eighth((y * 2 + core) * piece), 1, 0)
-    proj_other = along_tp(proj_out, 1, 0)
-    other_queries = across_x(queries)
-    gate, up_rows = gate_pre[0].T, up_pre[0].T
-    factor_other = gating_factor(jnp.stack([1 - x_lo]), gate, up_rows)
-    factor_own = gating_factor(jnp.stack([x_lo]), gate, up_rows)
+    def eighth(dy):
+        column = (((y + dy) % NY) * 2 + core) * piece
+        return lax.dynamic_slice(down_weight, (0, column), (units, piece))
+
+    first, second = together(eighth(0), eighth(2))
+    here = along_tp(first, 1, 0)
+    other_queries, proj_other = across_x(queries), across_x(proj_out)
 
     in_factor = jnp.dot(inputs[0], proj_in, preferred_element_type=F32).astype(BF16)
-    at_far, in_factor = together((((y + 2) % NY) * 2 + core) * piece, in_factor)
-    second = eighth(at_far)
     owners = owner_table[0, :, 0]
     ids = jnp.arange(count, dtype=jnp.int32)
     same = (owners[:, None] == owners[None, :]) & (ids[:, None] > ids[None, :])
@@ -301,31 +297,36 @@
         packed, "sc", split_axis=0, concat_axis=0, tiled=True, axis_index_groups=near
     )
 
-    here, arrived, factor_other, factor_own, second = together(
-        here, arrived, factor_other, factor_own, second
+    gate, up_rows = gate_pre[0].T, up_pre[0].T
+    factor_other = gating_factor(jnp.stack([1 - x_lo]), gate, up_rows)
+    factor_own = gating_factor(jnp.stack([x_lo]), gate, up_rows)
+
+    here, second, arrived, factor_other, factor_own = together(
+        here, second, arrived, factor_other, factor_own
     )
     before, after = along_sc(here, 1, 0), along_sc(here, -1, 0)
-    factor_other = along_tp(factor_other, 1, 0)
+    factor_other, far = along_tp(factor_other, 1, 0), across_x(second)
     mats = contract_queries(arrived, queries, other_queries)
-
-    factor_other, mats, second, proj_other = together(factor_other, mats, second, proj_other)
-    far = along_tp(second, 1, 0)
-    before, after, mats = together(before, after, mats)
-    held = [here, before, after, far]
-    flipped = [along_sc(a, 0, 1) for a in held]
     mats = lax.all_to_all(
         mats, "sc", split_axis=0, concat_axis=0, tiled=True, axis_index_groups=near
     )
-    at = jnp.stack([(y + dy) % NY for dy in (0, -1, 1, 2)] + [core]).astype(jnp.int32)
+    before, after, factor_other, far, proj_other = together(
+        before, after, factor_other, far, proj_other
+    )
+    weights = []
+    for a in (here, before, after, far):
+        weights += [a, along_sc(a, 0, 1)]
+
+    at = [(y + dy) % NY for dy in (0, -1, 1, 2)] + [core, 1 - core]
     parts = sum_units(
-        at,
+        jnp.stack(at).astype(jnp.int32),
         proj_out,
         proj_other,
         factor_own,
         factor_other,
+        down_weight,
         rows,
-        down_weight,
-        held + flipped,
+        weights,
     )
     parts, mats = together(parts, mats)
     parts = lax.all_to_all(

time: 127 us -> 114 us (0.90)
  waiting for transfers between devices: 54 us -> 43.9 us
  starting transfers between devices: 26.4 us -> 24.5 us
  Pallas kernels: 21.7 us -> 20 us
    ppermute x4 -> x2, waiting for transfers between devices: 41.1 us -> 10.3 us  [along_tp(): return lax.ppermute(a, 'tp', tp_perm(flip_x, dz))]
    ppermute x1 -> x3, waiting for transfers between devices: 0.01 us -> 16.4 us  [across_x(): return lax.ppermute(a, ('tp', 'sc'), pairs)]
    ppermute x1 -> x3, starting transfers between devices: 1.48 us -> 3.83 us  [across_x(): return lax.ppermute(a, ('tp', 'sc'), pairs)]
    ppermute x6, waiting for transfers between devices: 3.44 us -> 5.57 us  [along_sc(): return lax.ppermute(a, 'sc', sc_perm(dy, flip_core))]
    all_to_all x1, starting transfers between devices: 8.49 us -> 6.42 us  [body(): lax.all_to_all(parts, 'tp', split_axis=0, concat_axis=0, tiled=True, axis...]
    all_gather x1, waiting for transfers between devices: 0.01 us -> 2.07 us  [body(): lax.all_gather(rows_own, 'tp', axis=0, tiled=True, axis_index_groups=colu...]
    ppermute x4 -> x2, starting transfers between devices: 3.77 us -> 1.93 us  [along_tp(): return lax.ppermute(a, 'tp', tp_perm(flip_x, dz))]
  transfers between devices with their start and end apart: 15 -> 15, of which waited for: 7 -> 9; matrix products, arithmetic and copies ran while one was open for 5% -> 6% of each run, Pallas kernels for 16% -> 17%
where the time goes in v1:
time: 114 us; the launch traced here: 113 us
  waiting for transfers between devices  43.9 us (39%)
  starting transfers between devices  24.5 us (21%)
  Pallas kernels  20 us (18%)
  between operations  13.7 us (12%)
  local copies, waits for them, and re-layouts  8.6 us (8%)
  matrix products  2.31 us (2%)
    ppermute x3, waiting for transfers between devices, across_x(): return lax.ppermute(a, ('tp', 'sc'), pairs)  16.4 us
    pallas_call x1, Pallas kernels, sum_units(): pl.pallas_call(units_kernel, in_specs=[SMEM, VMEM, VMEM] + [HBM] * (4 + l...  13.5 us
    ppermute x2, waiting for transfers between devices, along_tp(): return lax.ppermute(a, 'tp', tp_perm(flip_x, dz))  10.3 us
    all_to_all x1, waiting for transfers between devices, body(): lax.all_to_all(parts, 'tp', split_axis=0, concat_axis=0, tiled=True, axis...  8.3 us
    all_to_all x1, starting transfers between devices, body(): lax.all_to_all(parts, 'tp', split_axis=0, concat_axis=0, tiled=True, axis...  6.42 us
    ppermute x6, waiting for transfers between devices, along_sc(): return lax.ppermute(a, 'sc', sc_perm(dy, flip_core))  5.57 us
    unnamed x23, local copies, waits for them, and re-layouts  4.74 us
    ppermute x6, starting transfers between devices, along_sc(): return lax.ppermute(a, 'sc', sc_perm(dy, flip_core))  4.33 us
  transfers between devices with their start and end apart: 15, of which 9 were waited for; matrix products, arithmetic and copies ran while one was open for 6% of the time, Pallas kernels for 17%

profile of v1, /device:TPU:6, one launch (start us, length us, event | category | flops | bytes accessed | tf_op | source)
XLA Modules:
  0.0 113.1 jit_solution(18293878715940271689)
XLA Ops:
  7.4 3.2 %constant_dynamic-slice_fusion = (bf16[800,640]{1,0:T(8,128)(2,1)}, bf16[800,640]{1,0:T(8,128)(2,1)}) fusion(bf16[800,5120]{1,0:T(8,128)(2,1)} %own_hbm.1, s32[]{:T(128)S(6)} %select_n.77, s32[]{:T(128)S(6)} %select_n.76), kind=kLoop, calls=%fused_computation.20 | loop fusion | bytes 4096008 | tf_op jit(solution)/shard_map/dynamic_slice | solution.py:274
  11.4 1.4 %collective-permute-start.10 = (bf16[128,4096]{1,0:T(8,128)(2,1)S(1)}, bf16[128,4096]{1,0:T(8,128)(2,1)}, u32[]{:S(2)}, u32[]{:S(2)}) collective-permute-start(bf16[128,4096]{1,0:T(8,128)(2,1)S(1)} %copy-done.5), channel_id=1, source_target_pairs={{0,136},{1,137},{2,138},{3,139},{4,140},{5,141},{6,142},{7,143},{8... | collective-permute-start | bytes 3145736 | tf_op jit(solution)/shard_map/ppermute | solution.py:44
  13.0 1.4 %convolution_convert_fusion.1 = bf16[64,64]{1,0:T(8,128)(2,1)S(1)} fusion(bf16[5120,64]{0,1:T(8,128)(2,1)S(1)} %copy-done, bf16[1,64,5120]{2,1,0:T(8,128)(2,1)} %param.10), kind=kOutput, calls=%fused_computation.1 | convolution fusion | flops 41947136 | bytes 1318912 | tf_op jit(solution)/shard_map/dot_general | solution.py:280
  14.4 0.9 convolution_convert_fusion
  15.3 4.2 %all-to-all-start = ((bf16[8,16,128]{2,1,0:T(8,128)(2,1)}), bf16[8,16,128]{2,1,0:T(8,128)(2,1)S(1)}, u32[]{:S(2)}, u32[]{:S(2)}) async-start(bf16[8,16,128]{2,1,0:T(8,128)(2,1)} %bitcast.8), calls=%async_computation | async-start | bytes 65536 | tf_op jit(solution)/shard_map/all_to_all | solution.py:296
  19.6 1.4 %copy-done.3 = bf16[1,1024,800]{1,2,0:T(8,128)(2,1)S(1)} copy-done((bf16[1,1024,800]{1,2,0:T(8,128)(2,1)S(1)}, bf16[1,1024,800]{1,2,0:T(8,128)(2,1)}, u32[]{:S(2)}) %copy-start.3) | copy-done | bytes 1638424
  25.0 10.3 %collective-permute-done.refs_0_ = bf16[800,640]{1,0:T(8,128)(2,1)} collective-permute-done((bf16[800,640]{1,0:T(8,128)(2,1)}, bf16[800,640]{1,0:T(8,128)(2,1)}, u32[]{:S(2)}, u32[]{:S(2)}) %collective-permute-start) | collective-permute-done | bytes 1024032 | tf_op jit(solution)/shard_map/ppermute | solution.py:31
  35.3 1.6 %collective-permute-start.1 = (bf16[800,640]{1,0:T(8,128)(2,1)}, bf16[800,640]{1,0:T(8,128)(2,1)}, u32[]{:S(2)}, u32[]{:S(2)}) collective-permute-start(bf16[800,640]{1,0:T(8,128)(2,1)} %collective-permute-done.refs_0_), channel_id=1, source_target_pairs={{0,2},{1,3},{2,4},{3,5},{4,6},{5,7},{6,0},{7,1},{8,10},{9,11},{10,... | collective-permute-start | bytes 3072008 | tf_op jit(solution)/shard_map/ppermute | solution.py:35
  36.8 1.7 %collective-permute-start.2 = (bf16[800,640]{1,0:T(8,128)(2,1)}, bf16[800,640]{1,0:T(8,128)(2,1)}, u32[]{:S(2)}, u32[]{:S(2)}) collective-permute-start(bf16[800,640]{1,0:T(8,128)(2,1)} %collective-permute-done.refs_0_), channel_id=1, source_target_pairs={{0,6},{1,7},{2,0},{3,1},{4,2},{5,3},{6,4},{7,5},{8,14},{9,15},{10,... | collective-permute-start | bytes 3072008 | tf_op jit(solution)/shard_map/ppermute | solution.py:35
  38.8 1.1 collective-permute-start.3
  39.9 3.6 %contract_queries.1 = bf16[128,8192]{1,0:T(8,128)(2,1)S(1)} custom-call(bf16[128,128]{1,0:T(8,128)(2,1)S(1)} %bitcast.35, bf16[128,4096]{1,0:T(8,128)(2,1)S(1)} %copy-done.5, bf16[128,4096]{1,0:T(8,128)(2,1)} %collective-permute-done.10.other_ref), custom_call_target="tpu_custom_call" | custom-call | flops 1000 | bytes 1000 | tf_op jit(solution)/shard_map/contract_queries/pallas_call | solution.py:83
  43.5 1.3 %copy-done.1 = bf16[128,8192]{1,0:T(8,128)(2,1)} copy-done((bf16[128,8192]{1,0:T(8,128)(2,1)}, bf16[128,8192]{1,0:T(8,128)(2,1)S(1)}, u32[]{:S(2)}) %copy-start.1) | copy-done | bytes 2097176
  44.8 3.7 %all-to-all-start.1 = ((bf16[8,16,8192]{2,1,0:T(8,128)(2,1)}), bf16[8,16,8192]{2,1,0:T(8,128)(2,1)S(1)}, u32[]{:S(2)}, u32[]{:S(2)}) async-start(bf16[8,16,8192]{2,1,0:T(8,128)(2,1)} %bitcast.29), calls=%async_computation.1 | async-start | bytes 4194304 | tf_op jit(solution)/shard_map/all_to_all | solution.py:310
  48.7 2.2 %collective-permute-start.5 = (bf16[800,64]{1,0:T(8,128)(2,1)S(1)}, bf16[800,64]{1,0:T(8,128)(2,1)S(1)}, u32[]{:S(2)}, u32[]{:S(2)}) collective-permute-start(bf16[800,64]{1,0:T(8,128)(2,1)S(1)} %copy.13.p_own), channel_id=1, source_target_pairs={{0,136},{1,137},{2,138},{3,139},{4,140},{5,141},{6,142},{7,143},{8... | collective-permute-start | bytes 307208 | tf_op jit(solution)/shard_map/ppermute | solution.py:44
  50.9 16.4 %collective-permute-done.5.p_other = bf16[800,64]{1,0:T(8,128)(2,1)S(1)} collective-permute-done((bf16[800,64]{1,0:T(8,128)(2,1)S(1)}, bf16[800,64]{1,0:T(8,128)(2,1)S(1)}, u32[]{:S(2)}, u32[]{:S(2)}) %collective-permute-start.5) | collective-permute-done | bytes 102432 | tf_op jit(solution)/shard_map/ppermute | solution.py:44
  69.1 1.2 %collective-permute-done.6.refs_1_ = bf16[800,640]{1,0:T(8,128)(2,1)} collective-permute-done((bf16[800,640]{1,0:T(8,128)(2,1)}, bf16[800,640]{1,0:T(8,128)(2,1)}, u32[]{:S(2)}, u32[]{:S(2)}) %collective-permute-start.6) | collective-permute-done | bytes 1024032 | tf_op jit(solution)/shard_map/ppermute | solution.py:35
  70.3 1.5 %collective-permute-done.7.refs_3_ = bf16[800,640]{1,0:T(8,128)(2,1)} collective-permute-done((bf16[800,640]{1,0:T(8,128)(2,1)}, bf16[800,640]{1,0:T(8,128)(2,1)}, u32[]{:S(2)}, u32[]{:S(2)}) %collective-permute-start.7) | collective-permute-done | bytes 1024032 | tf_op jit(solution)/shard_map/ppermute | solution.py:35
  71.7 1.5 %collective-permute-done.8.refs_5_ = bf16[800,640]{1,0:T(8,128)(2,1)} collective-permute-done((bf16[800,640]{1,0:T(8,128)(2,1)}, bf16[800,640]{1,0:T(8,128)(2,1)}, u32[]{:S(2)}, u32[]{:S(2)}) %collective-permute-start.8) | collective-permute-done | bytes 1024032 | tf_op jit(solution)/shard_map/ppermute | solution.py:35
  73.2 1.5 %collective-permute-done.9.refs_7_ = bf16[800,640]{1,0:T(8,128)(2,1)} collective-permute-done((bf16[800,640]{1,0:T(8,128)(2,1)}, bf16[800,640]{1,0:T(8,128)(2,1)}, u32[]{:S(2)}, u32[]{:S(2)}) %collective-permute-start.9) | collective-permute-done | bytes 1024032 | tf_op jit(solution)/shard_map/ppermute | solution.py:35
  74.7 2.1 %all-gather.3.cloned.1.call-done = bf16[1,512,5120]{2,1,0:T(8,128)(2,1)} async-done(((bf16[1,64,5120]{2,1,0:T(8,128)(2,1)}), bf16[1,512,5120]{2,1,0:T(8,128)(2,1)}) %all-gather.3.cloned.1.call-update) | async-done | bytes 5242896 | tf_op jit(solution)/shard_map/all_gather | solution.py:270
  76.7 13.5 %sum_units.1 = bf16[256,128]{1,0:T(8,128)(2,1)} custom-call(s32[6]{0:T(128)} %stack.33.at_ref, bf16[800,64]{1,0:T(8,128)(2,1)} %copy-done.7, bf16[800,64]{1,0:T(8,128)(2,1)} %copy-done.8, bf16[800,512]{1,0:T(8,128)(2,1)} %copy-done.4, bf16[800,512]{1,0:T(8,128)(2,1)} %collective-permute-done.3.f_other, bf16[800,5120]{1,0:T(8,128)(2,1)} %own_hbm.1, ...), custom_call_target="tpu_custom_call" | custom-call | flops 1000 | bytes 1000 | tf_op jit(solution)/shard_map/sum_units/pallas_call | solution.py:236
  90.3 6.4 %all-to-all-start.2 = ((bf16[8,32,128]{2,1,0:T(8,128)(2,1)}), bf16[8,32,128]{2,1,0:T(8,128)(2,1)S(1)}, u32[]{:S(2)}, u32[]{:S(2)}) async-start(bf16[8,32,128]{2,1,0:T(8,128)(2,1)} %bitcast.37), calls=%async_computation.2 | async-start | bytes 131072 | tf_op jit(solution)/shard_map/all_to_all | solution.py:332
  96.8 8.3 %all-to-all-done.2 = bf16[8,32,128]{2,1,0:T(8,128)(2,1)S(1)} async-done(((bf16[8,32,128]{2,1,0:T(8,128)(2,1)}), bf16[8,32,128]{2,1,0:T(8,128)(2,1)S(1)}, u32[]{:S(2)}, u32[]{:S(2)}) %all-to-all-start.2) | async-done | bytes 65568 | tf_op jit(solution)/shard_map/all_to_all | solution.py:332
  105.1 1.2 %score_rows.1 = f32[64,128]{1,0:T(8,128)} custom-call(bf16[64,128]{1,0:T(8,128)(2,1)S(1)} %fusion.1.place_ref, bf16[128,8192]{1,0:T(8,128)(2,1)S(1)} %bitcast.28, bf16[256,128]{1,0:T(8,128)(2,1)S(1)} %bitcast.34), custom_call_target="tpu_custom_call" | custom-call | flops 1000 | bytes 1000 | tf_op jit(solution)/shard_map/score_rows/pallas_call | solution.py:123
  (42 shorter events, 8.0 us)
Async XLA Ops:
  6.5 6.5 %copy-start = (bf16[5120,64]{0,1:T(8,128)(2,1)S(1)}, bf16[5120,64]{0,1:T(8,128)(2,1)}, u32[]{:S(2)}) copy-start(bf16[5120,64]{0,1:T(8,128)(2,1)} %param.14) | copy-start | bytes 1966084
  6.5 70.2 %all-gather.3.cloned.1.call-start = ((), (), s32[]{:S(2)}) async-start(), calls=%async_computation.3 | async-start | bytes 5898240 | tf_op jit(solution)/shard_map/all_gather | solution.py:270
  7.3 4.1 %copy-start.5 = (bf16[128,4096]{1,0:T(8,128)(2,1)S(1)}, bf16[128,4096]{1,0:T(8,128)(2,1)}, u32[]{:S(2)}) copy-start(bf16[128,4096]{1,0:T(8,128)(2,1)} %own_ref.1) | copy-start | bytes 3145732
  7.3 5.5 %copy-start.10 = (s32[1,64,1]{1,2,0:T(1,128)S(1)}, s32[1,64,1]{1,2,0:T(1,128)}, u32[]{:S(2)}) copy-start(s32[1,64,1]{1,2,0:T(1,128)} %param.17) | copy-start | bytes 772
  7.4 12.2 %copy-start.2 = (bf16[1,1024,800]{1,2,0:T(8,128)(2,1)S(1)}, bf16[1,1024,800]{1,2,0:T(8,128)(2,1)}, u32[]{:S(2)}) copy-start(bf16[1,1024,800]{1,2,0:T(8,128)(2,1)} %param.11) | copy-start | bytes 4915204
  10.6 24.7 %collective-permute-start = (bf16[800,640]{1,0:T(8,128)(2,1)}, bf16[800,640]{1,0:T(8,128)(2,1)}, u32[]{:S(2)}, u32[]{:S(2)}) collective-permute-start(bf16[800,640]{1,0:T(8,128)(2,1)} %get-tuple-element.19), channel_id=1, source_target_pairs={{0,128},{16,144},{32,160},{48,176},{64,192},{80,208},{96,224},{112... | collective-permute-start | bytes 3072008 | tf_op jit(solution)/shard_map/ppermute | solution.py:31
  11.4 28.5 %collective-permute-start.10 = (bf16[128,4096]{1,0:T(8,128)(2,1)S(1)}, bf16[128,4096]{1,0:T(8,128)(2,1)}, u32[]{:S(2)}, u32[]{:S(2)}) collective-permute-start(bf16[128,4096]{1,0:T(8,128)(2,1)S(1)} %copy-done.5), channel_id=1, source_target_pairs={{0,136},{1,137},{2,138},{3,139},{4,140},{5,141},{6,142},{7,143},{8... | collective-permute-start | bytes 3145736 | tf_op jit(solution)/shard_map/ppermute | solution.py:44
  15.3 9.7 %all-to-all-start = ((bf16[8,16,128]{2,1,0:T(8,128)(2,1)}), bf16[8,16,128]{2,1,0:T(8,128)(2,1)S(1)}, u32[]{:S(2)}, u32[]{:S(2)}) async-start(bf16[8,16,128]{2,1,0:T(8,128)(2,1)} %bitcast.8), calls=%async_computation | async-start | bytes 65536 | tf_op jit(solution)/shard_map/all_to_all | solution.py:296
  19.5 1.4 %copy-start.3 = (bf16[1,1024,800]{1,2,0:T(8,128)(2,1)S(1)}, bf16[1,1024,800]{1,2,0:T(8,128)(2,1)}, u32[]{:S(2)}) copy-start(bf16[1,1024,800]{1,2,0:T(8,128)(2,1)} %param.12) | copy-start | bytes 4915204
  35.3 32.1 %collective-permute-start.1 = (bf16[800,640]{1,0:T(8,128)(2,1)}, bf16[800,640]{1,0:T(8,128)(2,1)}, u32[]{:S(2)}, u32[]{:S(2)}) collective-permute-start(bf16[800,640]{1,0:T(8,128)(2,1)} %collective-permute-done.refs_0_), channel_id=1, source_target_pairs={{0,2},{1,3},{2,4},{3,5},{4,6},{5,7},{6,0},{7,1},{8,10},{9,11},{10,... | collective-permute-start | bytes 3072008 | tf_op jit(solution)/shard_map/ppermute | solution.py:35
  36.8 30.5 %collective-permute-start.2 = (bf16[800,640]{1,0:T(8,128)(2,1)}, bf16[800,640]{1,0:T(8,128)(2,1)}, u32[]{:S(2)}, u32[]{:S(2)}) collective-permute-start(bf16[800,640]{1,0:T(8,128)(2,1)} %collective-permute-done.refs_0_), channel_id=1, source_target_pairs={{0,6},{1,7},{2,0},{3,1},{4,2},{5,3},{6,4},{7,5},{8,14},{9,15},{10,... | collective-permute-start | bytes 3072008 | tf_op jit(solution)/shard_map/ppermute | solution.py:35
  38.5 28.8 %collective-permute-start.4 = (bf16[800,640]{1,0:T(8,128)(2,1)}, bf16[800,640]{1,0:T(8,128)(2,1)}, u32[]{:S(2)}, u32[]{:S(2)}) collective-permute-start(bf16[800,640]{1,0:T(8,128)(2,1)} %get-tuple-element.23), channel_id=1, source_target_pairs={{0,136},{1,137},{2,138},{3,139},{4,140},{5,141},{6,142},{7,143},{8... | collective-permute-start | bytes 3072008 | tf_op jit(solution)/shard_map/ppermute | solution.py:44
  38.8 28.6 %collective-permute-start.3 = (bf16[800,512]{1,0:T(8,128)(2,1)}, bf16[800,512]{1,0:T(8,128)(2,1)}, u32[]{:S(2)}, u32[]{:S(2)}) collective-permute-start(bf16[800,512]{1,0:T(8,128)(2,1)} %copy-done.6), channel_id=1, source_target_pairs={{0,128},{16,144},{32,160},{48,176},{64,192},{80,208},{96,224},{112... | collective-permute-start | bytes 2457608 | tf_op jit(solution)/shard_map/ppermute | solution.py:31
  43.5 1.3 %copy-start.1 = (bf16[128,8192]{1,0:T(8,128)(2,1)}, bf16[128,8192]{1,0:T(8,128)(2,1)S(1)}, u32[]{:S(2)}) copy-start(bf16[128,8192]{1,0:T(8,128)(2,1)S(1)} %contract_queries.1) | copy-start | bytes 6291460
  44.8 3.7 %copy-start.9 = (bf16[800,64]{0,1:T(8,128)(2,1)S(1)}, bf16[800,64]{0,1:T(8,128)(2,1)}, u32[]{:S(2)}) copy-start(bf16[800,64]{0,1:T(8,128)(2,1)} %param.15) | copy-start | bytes 307204
  44.8 45.5 %all-to-all-start.1 = ((bf16[8,16,8192]{2,1,0:T(8,128)(2,1)}), bf16[8,16,8192]{2,1,0:T(8,128)(2,1)S(1)}, u32[]{:S(2)}, u32[]{:S(2)}) async-start(bf16[8,16,8192]{2,1,0:T(8,128)(2,1)} %bitcast.29), calls=%async_computation.1 | async-start | bytes 4194304 | tf_op jit(solution)/shard_map/all_to_all | solution.py:310
  48.7 28.0 %copy-start.7 = (bf16[800,64]{1,0:T(8,128)(2,1)}, bf16[800,64]{1,0:T(8,128)(2,1)S(1)}, u32[]{:S(2)}) copy-start(bf16[800,64]{1,0:T(8,128)(2,1)S(1)} %copy.13.p_own) | copy-start | bytes 307204
  48.7 18.6 %collective-permute-start.5 = (bf16[800,64]{1,0:T(8,128)(2,1)S(1)}, bf16[800,64]{1,0:T(8,128)(2,1)S(1)}, u32[]{:S(2)}, u32[]{:S(2)}) collective-permute-start(bf16[800,64]{1,0:T(8,128)(2,1)S(1)} %copy.13.p_own), channel_id=1, source_target_pairs={{0,136},{1,137},{2,138},{3,139},{4,140},{5,141},{6,142},{7,143},{8... | collective-permute-start | bytes 307208 | tf_op jit(solution)/shard_map/ppermute | solution.py:44
  67.3 9.4 %copy-start.8 = (bf16[800,64]{1,0:T(8,128)(2,1)}, bf16[800,64]{1,0:T(8,128)(2,1)S(1)}, u32[]{:S(2)}) copy-start(bf16[800,64]{1,0:T(8,128)(2,1)S(1)} %collective-permute-done.5.p_other) | copy-start | bytes 307204
  67.3 3.0 %collective-permute-start.6 = (bf16[800,640]{1,0:T(8,128)(2,1)}, bf16[800,640]{1,0:T(8,128)(2,1)}, u32[]{:S(2)}, u32[]{:S(2)}) collective-permute-start(bf16[800,640]{1,0:T(8,128)(2,1)} %collective-permute-done.refs_0_), channel_id=1, source_target_pairs={{0,1},{1,0},{2,3},{3,2},{4,5},{5,4},{6,7},{7,6},{8,9},{9,8},{10,11... | collective-permute-start | bytes 3072008 | tf_op jit(solution)/shard_map/ppermute | solution.py:35
  67.3 4.4 %collective-permute-start.7 = (bf16[800,640]{1,0:T(8,128)(2,1)}, bf16[800,640]{1,0:T(8,128)(2,1)}, u32[]{:S(2)}, u32[]{:S(2)}) collective-permute-start(bf16[800,640]{1,0:T(8,128)(2,1)} %collective-permute-done.1.refs_2_), channel_id=1, source_target_pairs={{0,1},{1,0},{2,3},{3,2},{4,5},{5,4},{6,7},{7,6},{8,9},{9,8},{10,11... | collective-permute-start | bytes 3072008 | tf_op jit(solution)/shard_map/ppermute | solution.py:35
  67.9 5.3 %collective-permute-start.8 = (bf16[800,640]{1,0:T(8,128)(2,1)}, bf16[800,640]{1,0:T(8,128)(2,1)}, u32[]{:S(2)}, u32[]{:S(2)}) collective-permute-start(bf16[800,640]{1,0:T(8,128)(2,1)} %collective-permute-done.2.refs_4_), channel_id=1, source_target_pairs={{0,1},{1,0},{2,3},{3,2},{4,5},{5,4},{6,7},{7,6},{8,9},{9,8},{10,11... | collective-permute-start | bytes 3072008 | tf_op jit(solution)/shard_map/ppermute | solution.py:35
  68.0 6.6 %collective-permute-start.9 = (bf16[800,640]{1,0:T(8,128)(2,1)}, bf16[800,640]{1,0:T(8,128)(2,1)}, u32[]{:S(2)}, u32[]{:S(2)}) collective-permute-start(bf16[800,640]{1,0:T(8,128)(2,1)} %collective-permute-done.4.refs_6_), channel_id=1, source_target_pairs={{0,1},{1,0},{2,3},{3,2},{4,5},{5,4},{6,7},{7,6},{8,9},{9,8},{10,11... | collective-permute-start | bytes 3072008 | tf_op jit(solution)/shard_map/ppermute | solution.py:35
  90.3 14.8 %all-to-all-start.2 = ((bf16[8,32,128]{2,1,0:T(8,128)(2,1)}), bf16[8,32,128]{2,1,0:T(8,128)(2,1)S(1)}, u32[]{:S(2)}, u32[]{:S(2)}) async-start(bf16[8,32,128]{2,1,0:T(8,128)(2,1)} %bitcast.37), calls=%async_computation.2 | async-start | bytes 131072 | tf_op jit(solution)/shard_map/all_to_all | solution.py:332
  (2 other events, 1.8 us)
Sparse Core Ops, SparseCore 0:
  9.1 67.5 all-gather.2

commit v2 on v1

--- a/solution.py
+++ b/solution.py
@@ -96,7 +96,7 @@
     )(rows, own, other)
 
 
-def score_kernel(place_ref, mats_ref, parts_ref, out_ref):
+def score_kernel(mats_ref, parts_ref, out_ref):
     half = parts_ref.shape[0] // NZ
     total = parts_ref[:half, :].astype(F32)
     for n in range(1, NZ):
@@ -105,20 +105,15 @@
     total = jnp.concatenate([total[:, :count], total[:, count:]], axis=0)
     factor = total.astype(BF16).astype(F32).T
     queries = out_ref.shape[1]
-    step = 8 * queries
     score = jnp.zeros(out_ref.shape, F32)
-    for first in range(0, mats_ref.shape[1], step):
-        mats = jnp.dot(
-            place_ref[...], mats_ref[:, first : first + step], preferred_element_type=F32
-        )
-        for n in range(8):
-            i = first // queries + n
-            score = score + factor[:, i : i + 1] * mats[:, n * queries : (n + 1) * queries]
+    for i in range(factor.shape[1]):
+        mats = mats_ref[:, i * queries : (i + 1) * queries].astype(F32)
+        score = score + factor[:, i : i + 1] * mats
     out_ref[...] = score
 
 
-def score_rows(place, mats, parts):
-    rows = place.shape[0]
+def score_rows(mats, parts):
+    rows = mats.shape[0]
     queries = mats.shape[1] // (2 * parts.shape[0] // NZ)
     return pl.pallas_call(
         score_kernel,
@@ -126,7 +121,7 @@
         compiler_params=pltpu.CompilerParams(vmem_limit_bytes=16 * 1024 * 1024),
         cost_estimate=SMALL,
         name="score_rows",
-    )(place, mats, parts)
+    )(mats, parts)
 
 
 UNIT_STEPS = 5
@@ -332,7 +327,8 @@
     parts = lax.all_to_all(
         parts, "tp", split_axis=0, concat_axis=0, tiled=True, axis_index_groups=columns
     )
-    return score_rows(place, mats, parts)[None]
+    mats = jnp.dot(place, mats, preferred_element_type=F32).astype(BF16)
+    return score_rows(mats, parts)[None]
 
 
 def solution(mesh):

time: 114 us -> 115 us (level)
  matrix products: 2.31 us -> 4.38 us
  waiting for transfers between devices: 43.9 us -> 42.2 us
    dot_general x0 -> x1, matrix products: none -> 2.07 us  [body(): mats = jnp.dot(place, mats, preferred_element_type=F32).astype(BF16)]
    all_to_all x1, waiting for transfers between devices: 8.3 us -> 6.3 us  [body(): lax.all_to_all(parts, 'tp', split_axis=0, concat_axis=0, tiled=True, axis...]
    unnamed x23 -> x25, local copies, waits for them, and re-layouts: 4.74 us -> 4.76 us
  transfers between devices with their start and end apart: 15 -> 15, of which waited for: 9 -> 9; matrix products, arithmetic and copies ran while one was open for 6% -> 8% of each run, Pallas kernels for 17% -> 17%
where the time goes in v2:
time: 115 us; the launch traced here: 114 us
  waiting for transfers between devices  42.2 us (37%)
  starting transfers between devices  24.4 us (21%)
  Pallas kernels  21 us (18%)
  between operations  13.7 us (12%)
  local copies, waits for them, and re-layouts  8.62 us (7%)
  matrix products  4.38 us (4%)
    ppermute x3, waiting for transfers between devices, across_x(): return lax.ppermute(a, ('tp', 'sc'), pairs)  16.7 us
    pallas_call x1, Pallas kernels, sum_units(): pl.pallas_call(units_kernel, in_specs=[SMEM, VMEM, VMEM] + [HBM] * (4 + l...  13.5 us
    ppermute x2, waiting for transfers between devices, along_tp(): return lax.ppermute(a, 'tp', tp_perm(flip_x, dz))  10.3 us
    all_to_all x1, starting transfers between devices, body(): lax.all_to_all(parts, 'tp', split_axis=0, concat_axis=0, tiled=True, axis...  6.4 us
    all_to_all x1, waiting for transfers between devices, body(): lax.all_to_all(parts, 'tp', split_axis=0, concat_axis=0, tiled=True, axis...  6.3 us
    ppermute x6, waiting for transfers between devices, along_sc(): return lax.ppermute(a, 'sc', sc_perm(dy, flip_core))  5.55 us
    unnamed x25, local copies, waits for them, and re-layouts  4.76 us
    pallas_call x1, Pallas kernels, contract_queries(): pl.pallas_call(query_kernel, grid=(steps,), in_specs=[pl.BlockSpec((count...  4.62 us
  transfers between devices with their start and end apart: 15, of which 9 were waited for; matrix products, arithmetic and copies ran while one was open for 8% of the time, Pallas kernels for 17%

profile of v2, /device:TPU:6, one launch (start us, length us, event | category | flops | bytes accessed | tf_op | source)
XLA Modules:
  0.0 114.5 jit_solution(3473490432882466784)
XLA Ops:
  7.4 3.2 %constant_dynamic-slice_fusion = (bf16[800,640]{1,0:T(8,128)(2,1)}, bf16[800,640]{1,0:T(8,128)(2,1)}) fusion(bf16[800,5120]{1,0:T(8,128)(2,1)} %own_hbm.1, s32[]{:T(128)S(6)} %select_n.77, s32[]{:T(128)S(6)} %select_n.76), kind=kLoop, calls=%fused_computation.21 | loop fusion | bytes 4096008 | tf_op jit(solution)/shard_map/dynamic_slice | solution.py:269
  11.4 1.4 %collective-permute-start.10 = (bf16[128,4096]{1,0:T(8,128)(2,1)S(1)}, bf16[128,4096]{1,0:T(8,128)(2,1)}, u32[]{:S(2)}, u32[]{:S(2)}) collective-permute-start(bf16[128,4096]{1,0:T(8,128)(2,1)S(1)} %copy-done.5), channel_id=1, source_target_pairs={{0,136},{1,137},{2,138},{3,139},{4,140},{5,141},{6,142},{7,143},{8... | collective-permute-start | bytes 3145736 | tf_op jit(solution)/shard_map/ppermute | solution.py:44
  13.0 1.4 %convolution_convert_fusion.2 = bf16[64,64]{1,0:T(8,128)(2,1)S(1)} fusion(bf16[5120,64]{0,1:T(8,128)(2,1)S(1)} %copy-done, bf16[1,64,5120]{2,1,0:T(8,128)(2,1)} %param.10), kind=kOutput, calls=%fused_computation.2 | convolution fusion | flops 41947136 | bytes 1318912 | tf_op jit(solution)/shard_map/dot_general | solution.py:275
  15.3 4.2 %all-to-all-start = ((bf16[8,16,128]{2,1,0:T(8,128)(2,1)}), bf16[8,16,128]{2,1,0:T(8,128)(2,1)S(1)}, u32[]{:S(2)}, u32[]{:S(2)}) async-start(bf16[8,16,128]{2,1,0:T(8,128)(2,1)} %bitcast.8), calls=%async_computation | async-start | bytes 65536 | tf_op jit(solution)/shard_map/all_to_all | solution.py:291
  19.5 1.4 %copy-done.2 = bf16[1,1024,800]{1,2,0:T(8,128)(2,1)S(1)} copy-done((bf16[1,1024,800]{1,2,0:T(8,128)(2,1)S(1)}, bf16[1,1024,800]{1,2,0:T(8,128)(2,1)}, u32[]{:S(2)}) %copy-start.2) | copy-done | bytes 1638424
  25.0 10.3 %collective-permute-done.refs_0_ = bf16[800,640]{1,0:T(8,128)(2,1)} collective-permute-done((bf16[800,640]{1,0:T(8,128)(2,1)}, bf16[800,640]{1,0:T(8,128)(2,1)}, u32[]{:S(2)}, u32[]{:S(2)}) %collective-permute-start) | collective-permute-done | bytes 1024032 | tf_op jit(solution)/shard_map/ppermute | solution.py:31
  35.2 1.6 %collective-permute-start.1 = (bf16[800,640]{1,0:T(8,128)(2,1)}, bf16[800,640]{1,0:T(8,128)(2,1)}, u32[]{:S(2)}, u32[]{:S(2)}) collective-permute-start(bf16[800,640]{1,0:T(8,128)(2,1)} %collective-permute-done.refs_0_), channel_id=1, source_target_pairs={{0,2},{1,3},{2,4},{3,5},{4,6},{5,7},{6,0},{7,1},{8,10},{9,11},{10,... | collective-permute-start | bytes 3072008 | tf_op jit(solution)/shard_map/ppermute | solution.py:35
  36.8 1.7 %collective-permute-start.2 = (bf16[800,640]{1,0:T(8,128)(2,1)}, bf16[800,640]{1,0:T(8,128)(2,1)}, u32[]{:S(2)}, u32[]{:S(2)}) collective-permute-start(bf16[800,640]{1,0:T(8,128)(2,1)} %collective-permute-done.refs_0_), channel_id=1, source_target_pairs={{0,6},{1,7},{2,0},{3,1},{4,2},{5,3},{6,4},{7,5},{8,14},{9,15},{10,... | collective-permute-start | bytes 3072008 | tf_op jit(solution)/shard_map/ppermute | solution.py:35
  38.7 1.1 collective-permute-start.3
  39.9 4.6 %contract_queries.1 = bf16[128,8192]{1,0:T(8,128)(2,1)} custom-call(bf16[128,128]{1,0:T(8,128)(2,1)S(1)} %bitcast.34, bf16[128,4096]{1,0:T(8,128)(2,1)S(1)} %copy-done.5, bf16[128,4096]{1,0:T(8,128)(2,1)} %collective-permute-done.10.other_ref), custom_call_target="tpu_custom_call" | custom-call | flops 1000 | bytes 1000 | tf_op jit(solution)/shard_map/contract_queries/pallas_call | solution.py:83
  44.5 3.7 %all-to-all-start.1 = ((bf16[8,16,8192]{2,1,0:T(8,128)(2,1)}), bf16[8,16,8192]{2,1,0:T(8,128)(2,1)S(1)}, u32[]{:S(2)}, u32[]{:S(2)}) async-start(bf16[8,16,8192]{2,1,0:T(8,128)(2,1)} %bitcast.19), calls=%async_computation.1 | async-start | bytes 4194304 | tf_op jit(solution)/shard_map/all_to_all | solution.py:305
  48.4 2.2 %collective-permute-start.5 = (bf16[800,64]{1,0:T(8,128)(2,1)S(1)}, bf16[800,64]{1,0:T(8,128)(2,1)S(1)}, u32[]{:S(2)}, u32[]{:S(2)}) collective-permute-start(bf16[800,64]{1,0:T(8,128)(2,1)S(1)} %copy.13.p_own), channel_id=1, source_target_pairs={{0,136},{1,137},{2,138},{3,139},{4,140},{5,141},{6,142},{7,143},{8... | collective-permute-start | bytes 307208 | tf_op jit(solution)/shard_map/ppermute | solution.py:44
  50.6 16.7 %collective-permute-done.5.p_other = bf16[800,64]{1,0:T(8,128)(2,1)S(1)} collective-permute-done((bf16[800,64]{1,0:T(8,128)(2,1)S(1)}, bf16[800,64]{1,0:T(8,128)(2,1)S(1)}, u32[]{:S(2)}, u32[]{:S(2)}) %collective-permute-start.5) | collective-permute-done | bytes 102432 | tf_op jit(solution)/shard_map/ppermute | solution.py:44
  69.1 1.2 %collective-permute-done.6.refs_1_ = bf16[800,640]{1,0:T(8,128)(2,1)} collective-permute-done((bf16[800,640]{1,0:T(8,128)(2,1)}, bf16[800,640]{1,0:T(8,128)(2,1)}, u32[]{:S(2)}, u32[]{:S(2)}) %collective-permute-start.6) | collective-permute-done | bytes 1024032 | tf_op jit(solution)/shard_map/ppermute | solution.py:35
  70.3 1.5 %collective-permute-done.7.refs_3_ = bf16[800,640]{1,0:T(8,128)(2,1)} collective-permute-done((bf16[800,640]{1,0:T(8,128)(2,1)}, bf16[800,640]{1,0:T(8,128)(2,1)}, u32[]{:S(2)}, u32[]{:S(2)}) %collective-permute-start.7) | collective-permute-done | bytes 1024032 | tf_op jit(solution)/shard_map/ppermute | solution.py:35
  71.7 1.5 %collective-permute-done.8.refs_5_ = bf16[800,640]{1,0:T(8,128)(2,1)} collective-permute-done((bf16[800,640]{1,0:T(8,128)(2,1)}, bf16[800,640]{1,0:T(8,128)(2,1)}, u32[]{:S(2)}, u32[]{:S(2)}) %collective-permute-start.8) | collective-permute-done | bytes 1024032 | tf_op jit(solution)/shard_map/ppermute | solution.py:35
  73.2 1.5 %collective-permute-done.9.refs_7_ = bf16[800,640]{1,0:T(8,128)(2,1)} collective-permute-done((bf16[800,640]{1,0:T(8,128)(2,1)}, bf16[800,640]{1,0:T(8,128)(2,1)}, u32[]{:S(2)}, u32[]{:S(2)}) %collective-permute-start.9) | collective-permute-done | bytes 1024032 | tf_op jit(solution)/shard_map/ppermute | solution.py:35
  74.7 2.1 %all-gather.3.cloned.1.call-done = bf16[1,512,5120]{2,1,0:T(8,128)(2,1)} async-done(((bf16[1,64,5120]{2,1,0:T(8,128)(2,1)}), bf16[1,512,5120]{2,1,0:T(8,128)(2,1)}) %all-gather.3.cloned.1.call-update) | async-done | bytes 5242896 | tf_op jit(solution)/shard_map/all_gather | solution.py:265
  76.7 13.5 %sum_units.1 = bf16[256,128]{1,0:T(8,128)(2,1)} custom-call(s32[6]{0:T(128)} %stack.33.at_ref, bf16[800,64]{1,0:T(8,128)(2,1)} %copy-done.8, bf16[800,64]{1,0:T(8,128)(2,1)} %copy-done.9, bf16[800,512]{1,0:T(8,128)(2,1)} %copy-done.4, bf16[800,512]{1,0:T(8,128)(2,1)} %collective-permute-done.3.f_other, bf16[800,5120]{1,0:T(8,128)(2,1)} %own_hbm.1, ...), custom_call_target="tpu_custom_call" | custom-call | flops 1000 | bytes 1000 | tf_op jit(solution)/shard_map/sum_units/pallas_call | solution.py:231
  90.3 1.3 %copy-done.7 = bf16[8,16,8192]{2,1,0:T(8,128)(2,1)} copy-done((bf16[8,16,8192]{2,1,0:T(8,128)(2,1)}, bf16[8,16,8192]{2,1,0:T(8,128)(2,1)S(1)}, u32[]{:S(2)}) %copy-start.7) | copy-done | bytes 2097176
  91.6 6.4 %all-to-all-start.2 = ((bf16[8,32,128]{2,1,0:T(8,128)(2,1)}), bf16[8,32,128]{2,1,0:T(8,128)(2,1)S(1)}, u32[]{:S(2)}, u32[]{:S(2)}) async-start(bf16[8,32,128]{2,1,0:T(8,128)(2,1)} %bitcast.37), calls=%async_computation.2 | async-start | bytes 131072 | tf_op jit(solution)/shard_map/all_to_all | solution.py:327
  98.0 2.1 %convolution_convert_fusion.mats_ref = bf16[64,8192]{1,0:T(8,128)(2,1)S(1)} fusion(bf16[128,8192]{1,0:T(8,128)(2,1)} %bitcast.35, s32[64]{0:T(128)S(1)} %fusion.9), kind=kOutput, calls=%fused_computation | convolution fusion | flops 134750208 | bytes 3145984 | tf_op jit(solution)/shard_map/dot_general | solution.py:330
  100.1 6.3 %all-to-all-done.2 = bf16[8,32,128]{2,1,0:T(8,128)(2,1)S(1)} async-done(((bf16[8,32,128]{2,1,0:T(8,128)(2,1)}), bf16[8,32,128]{2,1,0:T(8,128)(2,1)S(1)}, u32[]{:S(2)}, u32[]{:S(2)}) %all-to-all-start.2) | async-done | bytes 65568 | tf_op jit(solution)/shard_map/all_to_all | solution.py:327
  106.4 1.2 %score_rows.1 = f32[64,128]{1,0:T(8,128)} custom-call(bf16[64,8192]{1,0:T(8,128)(2,1)S(1)} %convolution_convert_fusion.mats_ref, bf16[256,128]{1,0:T(8,128)(2,1)S(1)} %bitcast.33), custom_call_target="tpu_custom_call" | custom-call | flops 1000 | bytes 1000 | tf_op jit(solution)/shard_map/score_rows/pallas_call | solution.py:118
  (44 shorter events, 8.9 us)
Async XLA Ops:
  6.5 6.5 %copy-start = (bf16[5120,64]{0,1:T(8,128)(2,1)S(1)}, bf16[5120,64]{0,1:T(8,128)(2,1)}, u32[]{:S(2)}) copy-start(bf16[5120,64]{0,1:T(8,128)(2,1)} %param.14) | copy-start | bytes 1966084
  6.5 70.2 %all-gather.3.cloned.1.call-start = ((), (), s32[]{:S(2)}) async-start(), calls=%async_computation.3 | async-start | bytes 5898240 | tf_op jit(solution)/shard_map/all_gather | solution.py:265
  7.3 4.1 %copy-start.5 = (bf16[128,4096]{1,0:T(8,128)(2,1)S(1)}, bf16[128,4096]{1,0:T(8,128)(2,1)}, u32[]{:S(2)}) copy-start(bf16[128,4096]{1,0:T(8,128)(2,1)} %own_ref.1) | copy-start | bytes 3145732
  7.3 5.5 %copy-start.11 = (s32[1,64,1]{1,2,0:T(1,128)S(1)}, s32[1,64,1]{1,2,0:T(1,128)}, u32[]{:S(2)}) copy-start(s32[1,64,1]{1,2,0:T(1,128)} %param.17) | copy-start | bytes 772
  7.4 12.2 %copy-start.1 = (bf16[1,1024,800]{1,2,0:T(8,128)(2,1)S(1)}, bf16[1,1024,800]{1,2,0:T(8,128)(2,1)}, u32[]{:S(2)}) copy-start(bf16[1,1024,800]{1,2,0:T(8,128)(2,1)} %param.11) | copy-start | bytes 4915204
  10.6 24.7 %collective-permute-start = (bf16[800,640]{1,0:T(8,128)(2,1)}, bf16[800,640]{1,0:T(8,128)(2,1)}, u32[]{:S(2)}, u32[]{:S(2)}) collective-permute-start(bf16[800,640]{1,0:T(8,128)(2,1)} %get-tuple-element.19), channel_id=1, source_target_pairs={{0,128},{16,144},{32,160},{48,176},{64,192},{80,208},{96,224},{112... | collective-permute-start | bytes 3072008 | tf_op jit(solution)/shard_map/ppermute | solution.py:31
  11.4 28.5 %collective-permute-start.10 = (bf16[128,4096]{1,0:T(8,128)(2,1)S(1)}, bf16[128,4096]{1,0:T(8,128)(2,1)}, u32[]{:S(2)}, u32[]{:S(2)}) collective-permute-start(bf16[128,4096]{1,0:T(8,128)(2,1)S(1)} %copy-done.5), channel_id=1, source_target_pairs={{0,136},{1,137},{2,138},{3,139},{4,140},{5,141},{6,142},{7,143},{8... | collective-permute-start | bytes 3145736 | tf_op jit(solution)/shard_map/ppermute | solution.py:44
  15.3 9.7 %all-to-all-start = ((bf16[8,16,128]{2,1,0:T(8,128)(2,1)}), bf16[8,16,128]{2,1,0:T(8,128)(2,1)S(1)}, u32[]{:S(2)}, u32[]{:S(2)}) async-start(bf16[8,16,128]{2,1,0:T(8,128)(2,1)} %bitcast.8), calls=%async_computation | async-start | bytes 65536 | tf_op jit(solution)/shard_map/all_to_all | solution.py:291
  19.5 1.4 %copy-start.2 = (bf16[1,1024,800]{1,2,0:T(8,128)(2,1)S(1)}, bf16[1,1024,800]{1,2,0:T(8,128)(2,1)}, u32[]{:S(2)}) copy-start(bf16[1,1024,800]{1,2,0:T(8,128)(2,1)} %param.12) | copy-start | bytes 4915204
  21.0 1.7 %copy-start.3 = (bf16[1,1024,800]{1,2,0:T(8,128)(2,1)S(1)}, bf16[1,1024,800]{1,2,0:T(8,128)(2,1)}, u32[]{:S(2)}) copy-start(bf16[1,1024,800]{1,2,0:T(8,128)(2,1)} %param.12) | copy-start | bytes 4915204
  35.2 32.1 %collective-permute-start.1 = (bf16[800,640]{1,0:T(8,128)(2,1)}, bf16[800,640]{1,0:T(8,128)(2,1)}, u32[]{:S(2)}, u32[]{:S(2)}) collective-permute-start(bf16[800,640]{1,0:T(8,128)(2,1)} %collective-permute-done.refs_0_), channel_id=1, source_target_pairs={{0,2},{1,3},{2,4},{3,5},{4,6},{5,7},{6,0},{7,1},{8,10},{9,11},{10,... | collective-permute-start | bytes 3072008 | tf_op jit(solution)/shard_map/ppermute | solution.py:35
  36.8 30.5 %collective-permute-start.2 = (bf16[800,640]{1,0:T(8,128)(2,1)}, bf16[800,640]{1,0:T(8,128)(2,1)}, u32[]{:S(2)}, u32[]{:S(2)}) collective-permute-start(bf16[800,640]{1,0:T(8,128)(2,1)} %collective-permute-done.refs_0_), channel_id=1, source_target_pairs={{0,6},{1,7},{2,0},{3,1},{4,2},{5,3},{6,4},{7,5},{8,14},{9,15},{10,... | collective-permute-start | bytes 3072008 | tf_op jit(solution)/shard_map/ppermute | solution.py:35
  38.5 28.8 %collective-permute-start.4 = (bf16[800,640]{1,0:T(8,128)(2,1)}, bf16[800,640]{1,0:T(8,128)(2,1)}, u32[]{:S(2)}, u32[]{:S(2)}) collective-permute-start(bf16[800,640]{1,0:T(8,128)(2,1)} %get-tuple-element.23), channel_id=1, source_target_pairs={{0,136},{1,137},{2,138},{3,139},{4,140},{5,141},{6,142},{7,143},{8... | collective-permute-start | bytes 3072008 | tf_op jit(solution)/shard_map/ppermute | solution.py:44
  38.7 28.6 %collective-permute-start.3 = (bf16[800,512]{1,0:T(8,128)(2,1)}, bf16[800,512]{1,0:T(8,128)(2,1)}, u32[]{:S(2)}, u32[]{:S(2)}) collective-permute-start(bf16[800,512]{1,0:T(8,128)(2,1)} %copy-done.6), channel_id=1, source_target_pairs={{0,128},{16,144},{32,160},{48,176},{64,192},{80,208},{96,224},{112... | collective-permute-start | bytes 2457608 | tf_op jit(solution)/shard_map/ppermute | solution.py:31
  44.5 3.7 %copy-start.10 = (bf16[800,64]{0,1:T(8,128)(2,1)S(1)}, bf16[800,64]{0,1:T(8,128)(2,1)}, u32[]{:S(2)}) copy-start(bf16[800,64]{0,1:T(8,128)(2,1)} %param.15) | copy-start | bytes 307204
  44.5 45.8 %all-to-all-start.1 = ((bf16[8,16,8192]{2,1,0:T(8,128)(2,1)}), bf16[8,16,8192]{2,1,0:T(8,128)(2,1)S(1)}, u32[]{:S(2)}, u32[]{:S(2)}) async-start(bf16[8,16,8192]{2,1,0:T(8,128)(2,1)} %bitcast.19), calls=%async_computation.1 | async-start | bytes 4194304 | tf_op jit(solution)/shard_map/all_to_all | solution.py:305
  48.4 28.3 %copy-start.8 = (bf16[800,64]{1,0:T(8,128)(2,1)}, bf16[800,64]{1,0:T(8,128)(2,1)S(1)}, u32[]{:S(2)}) copy-start(bf16[800,64]{1,0:T(8,128)(2,1)S(1)} %copy.13.p_own) | copy-start | bytes 307204
  48.4 18.9 %collective-permute-start.5 = (bf16[800,64]{1,0:T(8,128)(2,1)S(1)}, bf16[800,64]{1,0:T(8,128)(2,1)S(1)}, u32[]{:S(2)}, u32[]{:S(2)}) collective-permute-start(bf16[800,64]{1,0:T(8,128)(2,1)S(1)} %copy.13.p_own), channel_id=1, source_target_pairs={{0,136},{1,137},{2,138},{3,139},{4,140},{5,141},{6,142},{7,143},{8... | collective-permute-start | bytes 307208 | tf_op jit(solution)/shard_map/ppermute | solution.py:44
  67.3 9.4 %copy-start.9 = (bf16[800,64]{1,0:T(8,128)(2,1)}, bf16[800,64]{1,0:T(8,128)(2,1)S(1)}, u32[]{:S(2)}) copy-start(bf16[800,64]{1,0:T(8,128)(2,1)S(1)} %collective-permute-done.5.p_other) | copy-start | bytes 307204
  67.3 3.0 %collective-permute-start.6 = (bf16[800,640]{1,0:T(8,128)(2,1)}, bf16[800,640]{1,0:T(8,128)(2,1)}, u32[]{:S(2)}, u32[]{:S(2)}) collective-permute-start(bf16[800,640]{1,0:T(8,128)(2,1)} %collective-permute-done.refs_0_), channel_id=1, source_target_pairs={{0,1},{1,0},{2,3},{3,2},{4,5},{5,4},{6,7},{7,6},{8,9},{9,8},{10,11... | collective-permute-start | bytes 3072008 | tf_op jit(solution)/shard_map/ppermute | solution.py:35
  67.3 4.4 %collective-permute-start.7 = (bf16[800,640]{1,0:T(8,128)(2,1)}, bf16[800,640]{1,0:T(8,128)(2,1)}, u32[]{:S(2)}, u32[]{:S(2)}) collective-permute-start(bf16[800,640]{1,0:T(8,128)(2,1)} %collective-permute-done.1.refs_2_), channel_id=1, source_target_pairs={{0,1},{1,0},{2,3},{3,2},{4,5},{5,4},{6,7},{7,6},{8,9},{9,8},{10,11... | collective-permute-start | bytes 3072008 | tf_op jit(solution)/shard_map/ppermute | solution.py:35
  67.9 5.3 %collective-permute-start.8 = (bf16[800,640]{1,0:T(8,128)(2,1)}, bf16[800,640]{1,0:T(8,128)(2,1)}, u32[]{:S(2)}, u32[]{:S(2)}) collective-permute-start(bf16[800,640]{1,0:T(8,128)(2,1)} %collective-permute-done.2.refs_4_), channel_id=1, source_target_pairs={{0,1},{1,0},{2,3},{3,2},{4,5},{5,4},{6,7},{7,6},{8,9},{9,8},{10,11... | collective-permute-start | bytes 3072008 | tf_op jit(solution)/shard_map/ppermute | solution.py:35
  68.0 6.6 %collective-permute-start.9 = (bf16[800,640]{1,0:T(8,128)(2,1)}, bf16[800,640]{1,0:T(8,128)(2,1)}, u32[]{:S(2)}, u32[]{:S(2)}) collective-permute-start(bf16[800,640]{1,0:T(8,128)(2,1)} %collective-permute-done.4.refs_6_), channel_id=1, source_target_pairs={{0,1},{1,0},{2,3},{3,2},{4,5},{5,4},{6,7},{7,6},{8,9},{9,8},{10,11... | collective-permute-start | bytes 3072008 | tf_op jit(solution)/shard_map/ppermute | solution.py:35
  91.6 14.8 %all-to-all-start.2 = ((bf16[8,32,128]{2,1,0:T(8,128)(2,1)}), bf16[8,32,128]{2,1,0:T(8,128)(2,1)S(1)}, u32[]{:S(2)}, u32[]{:S(2)}) async-start(bf16[8,32,128]{2,1,0:T(8,128)(2,1)} %bitcast.37), calls=%async_computation.2 | async-start | bytes 131072 | tf_op jit(solution)/shard_map/all_to_all | solution.py:327
  (3 other events, 3.2 us)
Sparse Core Ops, SparseCore 0:
  9.1 67.5 all-gather.2

commit v3 on v1

--- a/solution.py
+++ b/solution.py
@@ -310,11 +310,11 @@
     mats = lax.all_to_all(
         mats, "sc", split_axis=0, concat_axis=0, tiled=True, axis_index_groups=near
     )
-    before, after, factor_other, far, proj_other = together(
-        before, after, factor_other, far, proj_other
-    )
-    weights = []
-    for a in (here, before, after, far):
+    before, after, factor_other, far, proj_other, flipped = together(
+        before, after, factor_other, far, proj_other, along_sc(here, 0, 1)
+    )
+    weights = [here, flipped]
+    for a in (before, after, far):
         weights += [a, along_sc(a, 0, 1)]
 
     at = [(y + dy) % NY for dy in (0, -1, 1, 2)] + [core, 1 - core]

time: 114 us -> 112 us (0.982)
  starting transfers between devices: 24.5 us -> 21.5 us
    ppermute x3, waiting for transfers between devices: 16.4 us -> 5.46 us  [across_x(): return lax.ppermute(a, ('tp', 'sc'), pairs)]
    ppermute x2, waiting for transfers between devices: 10.3 us -> 15.6 us  [along_tp(): return lax.ppermute(a, 'tp', tp_perm(flip_x, dz))]
    all_gather x1, waiting for transfers between devices: 2.07 us -> 5.56 us  [body(): lax.all_gather(rows_own, 'tp', axis=0, tiled=True, axis_index_groups=colu...]
    ppermute x6, waiting for transfers between devices: 5.57 us -> 7.92 us  [along_sc(): return lax.ppermute(a, 'sc', sc_perm(dy, flip_core))]
    all_to_all x1, starting transfers between devices: 6.42 us -> 4.33 us  [body(): lax.all_to_all(parts, 'tp', split_axis=0, concat_axis=0, tiled=True, axis...]
    unnamed x23 -> x19, local copies, waits for them, and re-layouts: 4.74 us -> 5.49 us
  transfers between devices with their start and end apart: 15 -> 15, of which waited for: 9 -> 10; matrix products, arithmetic and copies ran while one was open for 6% -> 7% of each run, Pallas kernels for 17% -> 17%
where the time goes in v3:
time: 112 us; the launch traced here: 111 us
  waiting for transfers between devices  44 us (39%)
  starting transfers between devices  21.5 us (19%)
  Pallas kernels  20 us (18%)
  between operations  13.6 us (12%)
  local copies, waits for them, and re-layouts  9.36 us (8%)
  matrix products  2.3 us (2%)
    ppermute x2, waiting for transfers between devices, along_tp(): return lax.ppermute(a, 'tp', tp_perm(flip_x, dz))  15.6 us
    pallas_call x1, Pallas kernels, sum_units(): pl.pallas_call(units_kernel, in_specs=[SMEM, VMEM, VMEM] + [HBM] * (4 + l...  13.5 us
    all_to_all x1, waiting for transfers between devices, body(): lax.all_to_all(parts, 'tp', split_axis=0, concat_axis=0, tiled=True, axis...  8.3 us
    ppermute x6, waiting for transfers between devices, along_sc(): return lax.ppermute(a, 'sc', sc_perm(dy, flip_core))  7.92 us
    all_gather x1, waiting for transfers between devices, body(): lax.all_gather(rows_own, 'tp', axis=0, tiled=True, axis_index_groups=colu...  5.56 us
    unnamed x19, local copies, waits for them, and re-layouts  5.49 us
    ppermute x3, waiting for transfers between devices, across_x(): return lax.ppermute(a, ('tp', 'sc'), pairs)  5.46 us
    all_to_all x1, starting transfers between devices, body(): lax.all_to_all(packed, 'sc', split_axis=0, concat_axis=0, tiled=True, axi...  4.47 us
  transfers between devices with their start and end apart: 15, of which 10 were waited for; matrix products, arithmetic and copies ran while one was open for 7% of the time, Pallas kernels for 17%

profile of v3, /device:TPU:6, one launch (start us, length us, event | category | flops | bytes accessed | tf_op | source)
XLA Modules:
  0.0 111.1 jit_solution(13669570819213625357)
XLA Ops:
  7.4 3.2 %constant_dynamic-slice_fusion = (bf16[800,640]{1,0:T(8,128)(2,1)}, bf16[800,640]{1,0:T(8,128)(2,1)}) fusion(bf16[800,5120]{1,0:T(8,128)(2,1)} %own_hbm.1, s32[]{:T(128)S(6)} %select_n.77, s32[]{:T(128)S(6)} %select_n.76), kind=kLoop, calls=%fused_computation.20 | loop fusion | bytes 4096008 | tf_op jit(solution)/shard_map/dynamic_slice | solution.py:274
  12.2 1.4 %collective-permute-start.5 = (bf16[800,64]{1,0:T(8,128)(2,1)}, bf16[800,64]{1,0:T(8,128)(2,1)}, u32[]{:S(2)}, u32[]{:S(2)}) collective-permute-start(bf16[800,64]{1,0:T(8,128)(2,1)} %copy.13.p_own), channel_id=1, source_target_pairs={{0,136},{1,137},{2,138},{3,139},{4,140},{5,141},{6,142},{7,143},{8... | collective-permute-start | bytes 307208 | tf_op jit(solution)/shard_map/ppermute | solution.py:44
  13.6 1.8 %collective-permute-start.10 = (bf16[128,4096]{1,0:T(8,128)(2,1)S(1)}, bf16[128,4096]{1,0:T(8,128)(2,1)}, u32[]{:S(2)}, u32[]{:S(2)}) collective-permute-start(bf16[128,4096]{1,0:T(8,128)(2,1)S(1)} %copy-done.5), channel_id=1, source_target_pairs={{0,136},{1,137},{2,138},{3,139},{4,140},{5,141},{6,142},{7,143},{8... | collective-permute-start | bytes 3145736 | tf_op jit(solution)/shard_map/ppermute | solution.py:44
  15.7 1.4 %convolution_convert_fusion.1 = bf16[64,64]{1,0:T(8,128)(2,1)S(1)} fusion(bf16[5120,64]{0,1:T(8,128)(2,1)S(1)} %copy-done, bf16[1,64,5120]{2,1,0:T(8,128)(2,1)} %param.10), kind=kOutput, calls=%fused_computation.1 | convolution fusion | flops 41947136 | bytes 1318912 | tf_op jit(solution)/shard_map/dot_general | solution.py:280
  18.0 4.5 %all-to-all-start = ((bf16[8,16,128]{2,1,0:T(8,128)(2,1)}), bf16[8,16,128]{2,1,0:T(8,128)(2,1)S(1)}, u32[]{:S(2)}, u32[]{:S(2)}) async-start(bf16[8,16,128]{2,1,0:T(8,128)(2,1)} %bitcast.8), calls=%async_computation | async-start | bytes 65536 | tf_op jit(solution)/shard_map/all_to_all | solution.py:296
  22.5 1.5 %copy-done.3 = bf16[1,1024,800]{1,2,0:T(8,128)(2,1)S(1)} copy-done((bf16[1,1024,800]{1,2,0:T(8,128)(2,1)S(1)}, bf16[1,1024,800]{1,2,0:T(8,128)(2,1)}, u32[]{:S(2)}) %copy-start.3) | copy-done | bytes 1638424
  24.9 0.9 copy-done.6
  27.9 7.4 %collective-permute-done.refs_0_ = bf16[800,640]{1,0:T(8,128)(2,1)} collective-permute-done((bf16[800,640]{1,0:T(8,128)(2,1)}, bf16[800,640]{1,0:T(8,128)(2,1)}, u32[]{:S(2)}, u32[]{:S(2)}) %collective-permute-start) | collective-permute-done | bytes 1024032 | tf_op jit(solution)/shard_map/ppermute | solution.py:31
  35.3 1.6 %collective-permute-start.1 = (bf16[800,640]{1,0:T(8,128)(2,1)}, bf16[800,640]{1,0:T(8,128)(2,1)}, u32[]{:S(2)}, u32[]{:S(2)}) collective-permute-start(bf16[800,640]{1,0:T(8,128)(2,1)} %collective-permute-done.refs_0_), channel_id=1, source_target_pairs={{0,2},{1,3},{2,4},{3,5},{4,6},{5,7},{6,0},{7,1},{8,10},{9,11},{10,... | collective-permute-start | bytes 3072008 | tf_op jit(solution)/shard_map/ppermute | solution.py:35
  36.9 1.7 %collective-permute-start.2 = (bf16[800,640]{1,0:T(8,128)(2,1)}, bf16[800,640]{1,0:T(8,128)(2,1)}, u32[]{:S(2)}, u32[]{:S(2)}) collective-permute-start(bf16[800,640]{1,0:T(8,128)(2,1)} %collective-permute-done.refs_0_), channel_id=1, source_target_pairs={{0,6},{1,7},{2,0},{3,1},{4,2},{5,3},{6,4},{7,5},{8,14},{9,15},{10,... | collective-permute-start | bytes 3072008 | tf_op jit(solution)/shard_map/ppermute | solution.py:35
  38.8 5.5 %collective-permute-done.10.other_ref = bf16[128,4096]{1,0:T(8,128)(2,1)} collective-permute-done((bf16[128,4096]{1,0:T(8,128)(2,1)S(1)}, bf16[128,4096]{1,0:T(8,128)(2,1)}, u32[]{:S(2)}, u32[]{:S(2)}) %collective-permute-start.10) | collective-permute-done | bytes 1048608 | tf_op jit(solution)/shard_map/ppermute | solution.py:44
  44.2 3.6 %contract_queries.1 = bf16[128,8192]{1,0:T(8,128)(2,1)S(1)} custom-call(bf16[128,128]{1,0:T(8,128)(2,1)S(1)} %bitcast.35, bf16[128,4096]{1,0:T(8,128)(2,1)S(1)} %copy-done.5, bf16[128,4096]{1,0:T(8,128)(2,1)} %collective-permute-done.10.other_ref), custom_call_target="tpu_custom_call" | custom-call | flops 1000 | bytes 1000 | tf_op jit(solution)/shard_map/contract_queries/pallas_call | solution.py:83
  47.9 1.3 %copy-done.1 = bf16[128,8192]{1,0:T(8,128)(2,1)} copy-done((bf16[128,8192]{1,0:T(8,128)(2,1)}, bf16[128,8192]{1,0:T(8,128)(2,1)S(1)}, u32[]{:S(2)}) %copy-start.1) | copy-done | bytes 2097176
  49.2 4.5 %all-to-all-start.1 = ((bf16[8,16,8192]{2,1,0:T(8,128)(2,1)}), bf16[8,16,8192]{2,1,0:T(8,128)(2,1)S(1)}, u32[]{:S(2)}, u32[]{:S(2)}) async-start(bf16[8,16,8192]{2,1,0:T(8,128)(2,1)} %bitcast.29), calls=%async_computation.1 | async-start | bytes 4194304 | tf_op jit(solution)/shard_map/all_to_all | solution.py:310
  53.6 8.2 %collective-permute-done.3.f_other = bf16[800,512]{1,0:T(8,128)(2,1)} collective-permute-done((bf16[800,512]{1,0:T(8,128)(2,1)}, bf16[800,512]{1,0:T(8,128)(2,1)}, u32[]{:S(2)}, u32[]{:S(2)}) %collective-permute-start.3) | collective-permute-done | bytes 819232 | tf_op jit(solution)/shard_map/ppermute | solution.py:31
  61.9 3.3 %collective-permute-done.1.refs_2_ = bf16[800,640]{1,0:T(8,128)(2,1)} collective-permute-done((bf16[800,640]{1,0:T(8,128)(2,1)}, bf16[800,640]{1,0:T(8,128)(2,1)}, u32[]{:S(2)}, u32[]{:S(2)}) %collective-permute-start.1) | collective-permute-done | bytes 1024032 | tf_op jit(solution)/shard_map/ppermute | solution.py:35
  66.6 1.7 %collective-permute-done.7.refs_3_ = bf16[800,640]{1,0:T(8,128)(2,1)} collective-permute-done((bf16[800,640]{1,0:T(8,128)(2,1)}, bf16[800,640]{1,0:T(8,128)(2,1)}, u32[]{:S(2)}, u32[]{:S(2)}) %collective-permute-start.7) | collective-permute-done | bytes 1024032 | tf_op jit(solution)/shard_map/ppermute | solution.py:35
  68.2 1.5 %collective-permute-done.8.refs_5_ = bf16[800,640]{1,0:T(8,128)(2,1)} collective-permute-done((bf16[800,640]{1,0:T(8,128)(2,1)}, bf16[800,640]{1,0:T(8,128)(2,1)}, u32[]{:S(2)}, u32[]{:S(2)}) %collective-permute-start.8) | collective-permute-done | bytes 1024032 | tf_op jit(solution)/shard_map/ppermute | solution.py:35
  69.7 1.5 %collective-permute-done.9.refs_7_ = bf16[800,640]{1,0:T(8,128)(2,1)} collective-permute-done((bf16[800,640]{1,0:T(8,128)(2,1)}, bf16[800,640]{1,0:T(8,128)(2,1)}, u32[]{:S(2)}, u32[]{:S(2)}) %collective-permute-start.9) | collective-permute-done | bytes 1024032 | tf_op jit(solution)/shard_map/ppermute | solution.py:35
  71.2 5.6 %all-gather.3.cloned.1.call-done = bf16[1,512,5120]{2,1,0:T(8,128)(2,1)} async-done(((bf16[1,64,5120]{2,1,0:T(8,128)(2,1)}), bf16[1,512,5120]{2,1,0:T(8,128)(2,1)}) %all-gather.3.cloned.1.call-update) | async-done | bytes 5242896 | tf_op jit(solution)/shard_map/all_gather | solution.py:270
  76.7 13.5 %sum_units.1 = bf16[256,128]{1,0:T(8,128)(2,1)} custom-call(s32[6]{0:T(128)} %stack.33.at_ref, bf16[800,64]{1,0:T(8,128)(2,1)} %copy.13.p_own, bf16[800,64]{1,0:T(8,128)(2,1)} %collective-permute-done.5.p_other, bf16[800,512]{1,0:T(8,128)(2,1)} %copy-done.4, bf16[800,512]{1,0:T(8,128)(2,1)} %collective-permute-done.3.f_other, bf16[800,5120]{1,0:T(8,128)(2,1)} %own_hbm.1, ...), custom_call_target="tpu_custom_call" | custom-call | flops 1000 | bytes 1000 | tf_op jit(solution)/shard_map/sum_units/pallas_call | solution.py:236
  90.3 4.3 %all-to-all-start.2 = ((bf16[8,32,128]{2,1,0:T(8,128)(2,1)}), bf16[8,32,128]{2,1,0:T(8,128)(2,1)S(1)}, u32[]{:S(2)}, u32[]{:S(2)}) async-start(bf16[8,32,128]{2,1,0:T(8,128)(2,1)} %bitcast.37), calls=%async_computation.2 | async-start | bytes 131072 | tf_op jit(solution)/shard_map/all_to_all | solution.py:332
  94.7 8.3 %all-to-all-done.2 = bf16[8,32,128]{2,1,0:T(8,128)(2,1)S(1)} async-done(((bf16[8,32,128]{2,1,0:T(8,128)(2,1)}), bf16[8,32,128]{2,1,0:T(8,128)(2,1)S(1)}, u32[]{:S(2)}, u32[]{:S(2)}) %all-to-all-start.2) | async-done | bytes 65568 | tf_op jit(solution)/shard_map/all_to_all | solution.py:332
  103.0 1.2 %score_rows.1 = f32[64,128]{1,0:T(8,128)} custom-call(bf16[64,128]{1,0:T(8,128)(2,1)S(1)} %fusion.1.place_ref, bf16[128,8192]{1,0:T(8,128)(2,1)S(1)} %bitcast.28, bf16[256,128]{1,0:T(8,128)(2,1)S(1)} %bitcast.34), custom_call_target="tpu_custom_call" | custom-call | flops 1000 | bytes 1000 | tf_op jit(solution)/shard_map/score_rows/pallas_call | solution.py:123
  (38 shorter events, 8.1 us)
Async XLA Ops:
  6.5 9.1 %copy-start = (bf16[5120,64]{0,1:T(8,128)(2,1)S(1)}, bf16[5120,64]{0,1:T(8,128)(2,1)}, u32[]{:S(2)}) copy-start(bf16[5120,64]{0,1:T(8,128)(2,1)} %param.14) | copy-start | bytes 1966084
  6.5 70.2 %all-gather.3.cloned.1.call-start = ((), (), s32[]{:S(2)}) async-start(), calls=%async_computation.3 | async-start | bytes 5898240 | tf_op jit(solution)/shard_map/all_gather | solution.py:270
  7.3 4.1 %copy-start.7 = (bf16[800,64]{0,1:T(8,128)(2,1)S(1)}, bf16[800,64]{0,1:T(8,128)(2,1)}, u32[]{:S(2)}) copy-start(bf16[800,64]{0,1:T(8,128)(2,1)} %param.15) | copy-start | bytes 307204
  7.4 6.3 %copy-start.5 = (bf16[128,4096]{1,0:T(8,128)(2,1)S(1)}, bf16[128,4096]{1,0:T(8,128)(2,1)}, u32[]{:S(2)}) copy-start(bf16[128,4096]{1,0:T(8,128)(2,1)} %own_ref.1) | copy-start | bytes 3145732
  7.4 8.1 %copy-start.8 = (s32[1,64,1]{1,2,0:T(1,128)S(1)}, s32[1,64,1]{1,2,0:T(1,128)}, u32[]{:S(2)}) copy-start(s32[1,64,1]{1,2,0:T(1,128)} %param.17) | copy-start | bytes 772
  7.4 15.1 %copy-start.2 = (bf16[1,1024,800]{1,2,0:T(8,128)(2,1)S(1)}, bf16[1,1024,800]{1,2,0:T(8,128)(2,1)}, u32[]{:S(2)}) copy-start(bf16[1,1024,800]{1,2,0:T(8,128)(2,1)} %param.11) | copy-start | bytes 4915204
  10.6 24.7 %collective-permute-start = (bf16[800,640]{1,0:T(8,128)(2,1)}, bf16[800,640]{1,0:T(8,128)(2,1)}, u32[]{:S(2)}, u32[]{:S(2)}) collective-permute-start(bf16[800,640]{1,0:T(8,128)(2,1)} %get-tuple-element.20), channel_id=1, source_target_pairs={{0,128},{16,144},{32,160},{48,176},{64,192},{80,208},{96,224},{112... | collective-permute-start | bytes 3072008 | tf_op jit(solution)/shard_map/ppermute | solution.py:31
  12.2 26.5 %collective-permute-start.5 = (bf16[800,64]{1,0:T(8,128)(2,1)}, bf16[800,64]{1,0:T(8,128)(2,1)}, u32[]{:S(2)}, u32[]{:S(2)}) collective-permute-start(bf16[800,64]{1,0:T(8,128)(2,1)} %copy.13.p_own), channel_id=1, source_target_pairs={{0,136},{1,137},{2,138},{3,139},{4,140},{5,141},{6,142},{7,143},{8... | collective-permute-start | bytes 307208 | tf_op jit(solution)/shard_map/ppermute | solution.py:44
  13.6 30.6 %collective-permute-start.10 = (bf16[128,4096]{1,0:T(8,128)(2,1)S(1)}, bf16[128,4096]{1,0:T(8,128)(2,1)}, u32[]{:S(2)}, u32[]{:S(2)}) collective-permute-start(bf16[128,4096]{1,0:T(8,128)(2,1)S(1)} %copy-done.5), channel_id=1, source_target_pairs={{0,136},{1,137},{2,138},{3,139},{4,140},{5,141},{6,142},{7,143},{8... | collective-permute-start | bytes 3145736 | tf_op jit(solution)/shard_map/ppermute | solution.py:44
  18.0 9.9 %all-to-all-start = ((bf16[8,16,128]{2,1,0:T(8,128)(2,1)}), bf16[8,16,128]{2,1,0:T(8,128)(2,1)S(1)}, u32[]{:S(2)}, u32[]{:S(2)}) async-start(bf16[8,16,128]{2,1,0:T(8,128)(2,1)} %bitcast.8), calls=%async_computation | async-start | bytes 65536 | tf_op jit(solution)/shard_map/all_to_all | solution.py:296
  22.5 1.5 %copy-start.3 = (bf16[1,1024,800]{1,2,0:T(8,128)(2,1)S(1)}, bf16[1,1024,800]{1,2,0:T(8,128)(2,1)}, u32[]{:S(2)}) copy-start(bf16[1,1024,800]{1,2,0:T(8,128)(2,1)} %param.12) | copy-start | bytes 4915204
  24.8 0.9 copy-start.6
  26.6 0.9 copy-start.4
  35.3 29.9 %collective-permute-start.1 = (bf16[800,640]{1,0:T(8,128)(2,1)}, bf16[800,640]{1,0:T(8,128)(2,1)}, u32[]{:S(2)}, u32[]{:S(2)}) collective-permute-start(bf16[800,640]{1,0:T(8,128)(2,1)} %collective-permute-done.refs_0_), channel_id=1, source_target_pairs={{0,2},{1,3},{2,4},{3,5},{4,6},{5,7},{6,0},{7,1},{8,10},{9,11},{10,... | collective-permute-start | bytes 3072008 | tf_op jit(solution)/shard_map/ppermute | solution.py:35
  36.9 28.3 %collective-permute-start.2 = (bf16[800,640]{1,0:T(8,128)(2,1)}, bf16[800,640]{1,0:T(8,128)(2,1)}, u32[]{:S(2)}, u32[]{:S(2)}) collective-permute-start(bf16[800,640]{1,0:T(8,128)(2,1)} %collective-permute-done.refs_0_), channel_id=1, source_target_pairs={{0,6},{1,7},{2,0},{3,1},{4,2},{5,3},{6,4},{7,5},{8,14},{9,15},{10,... | collective-permute-start | bytes 3072008 | tf_op jit(solution)/shard_map/ppermute | solution.py:35
  38.5 26.7 %collective-permute-start.4 = (bf16[800,640]{1,0:T(8,128)(2,1)}, bf16[800,640]{1,0:T(8,128)(2,1)}, u32[]{:S(2)}, u32[]{:S(2)}) collective-permute-start(bf16[800,640]{1,0:T(8,128)(2,1)} %get-tuple-element.24), channel_id=1, source_target_pairs={{0,136},{1,137},{2,138},{3,139},{4,140},{5,141},{6,142},{7,143},{8... | collective-permute-start | bytes 3072008 | tf_op jit(solution)/shard_map/ppermute | solution.py:44
  38.8 26.4 %collective-permute-start.6 = (bf16[800,640]{1,0:T(8,128)(2,1)}, bf16[800,640]{1,0:T(8,128)(2,1)}, u32[]{:S(2)}, u32[]{:S(2)}) collective-permute-start(bf16[800,640]{1,0:T(8,128)(2,1)} %collective-permute-done.refs_0_), channel_id=1, source_target_pairs={{0,1},{1,0},{2,3},{3,2},{4,5},{5,4},{6,7},{7,6},{8,9},{9,8},{10,11... | collective-permute-start | bytes 3072008 | tf_op jit(solution)/shard_map/ppermute | solution.py:35
  44.2 17.6 %collective-permute-start.3 = (bf16[800,512]{1,0:T(8,128)(2,1)}, bf16[800,512]{1,0:T(8,128)(2,1)}, u32[]{:S(2)}, u32[]{:S(2)}) collective-permute-start(bf16[800,512]{1,0:T(8,128)(2,1)} %copy-done.6), channel_id=1, source_target_pairs={{0,128},{16,144},{32,160},{48,176},{64,192},{80,208},{96,224},{112... | collective-permute-start | bytes 2457608 | tf_op jit(solution)/shard_map/ppermute | solution.py:31
  47.8 1.3 %copy-start.1 = (bf16[128,8192]{1,0:T(8,128)(2,1)}, bf16[128,8192]{1,0:T(8,128)(2,1)S(1)}, u32[]{:S(2)}) copy-start(bf16[128,8192]{1,0:T(8,128)(2,1)S(1)} %contract_queries.1) | copy-start | bytes 6291460
  49.2 41.1 %all-to-all-start.1 = ((bf16[8,16,8192]{2,1,0:T(8,128)(2,1)}), bf16[8,16,8192]{2,1,0:T(8,128)(2,1)S(1)}, u32[]{:S(2)}, u32[]{:S(2)}) async-start(bf16[8,16,8192]{2,1,0:T(8,128)(2,1)} %bitcast.29), calls=%async_computation.1 | async-start | bytes 4194304 | tf_op jit(solution)/shard_map/all_to_all | solution.py:310
  65.2 3.1 %collective-permute-start.7 = (bf16[800,640]{1,0:T(8,128)(2,1)}, bf16[800,640]{1,0:T(8,128)(2,1)}, u32[]{:S(2)}, u32[]{:S(2)}) collective-permute-start(bf16[800,640]{1,0:T(8,128)(2,1)} %collective-permute-done.1.refs_2_), channel_id=1, source_target_pairs={{0,1},{1,0},{2,3},{3,2},{4,5},{5,4},{6,7},{7,6},{8,9},{9,8},{10,11... | collective-permute-start | bytes 3072008 | tf_op jit(solution)/shard_map/ppermute | solution.py:35
  65.3 4.4 %collective-permute-start.8 = (bf16[800,640]{1,0:T(8,128)(2,1)}, bf16[800,640]{1,0:T(8,128)(2,1)}, u32[]{:S(2)}, u32[]{:S(2)}) collective-permute-start(bf16[800,640]{1,0:T(8,128)(2,1)} %collective-permute-done.2.refs_4_), channel_id=1, source_target_pairs={{0,1},{1,0},{2,3},{3,2},{4,5},{5,4},{6,7},{7,6},{8,9},{9,8},{10,11... | collective-permute-start | bytes 3072008 | tf_op jit(solution)/shard_map/ppermute | solution.py:35
  65.8 5.4 %collective-permute-start.9 = (bf16[800,640]{1,0:T(8,128)(2,1)}, bf16[800,640]{1,0:T(8,128)(2,1)}, u32[]{:S(2)}, u32[]{:S(2)}) collective-permute-start(bf16[800,640]{1,0:T(8,128)(2,1)} %collective-permute-done.4.refs_6_), channel_id=1, source_target_pairs={{0,1},{1,0},{2,3},{3,2},{4,5},{5,4},{6,7},{7,6},{8,9},{9,8},{10,11... | collective-permute-start | bytes 3072008 | tf_op jit(solution)/shard_map/ppermute | solution.py:35
  90.3 12.7 %all-to-all-start.2 = ((bf16[8,32,128]{2,1,0:T(8,128)(2,1)}), bf16[8,32,128]{2,1,0:T(8,128)(2,1)S(1)}, u32[]{:S(2)}, u32[]{:S(2)}) async-start(bf16[8,32,128]{2,1,0:T(8,128)(2,1)} %bitcast.37), calls=%async_computation.2 | async-start | bytes 131072 | tf_op jit(solution)/shard_map/all_to_all | solution.py:332
Sparse Core Ops, SparseCore 0:
  9.1 67.5 all-gather.2
